TPU v7x, 128 devices: a whole 4x4x4 slice. The times are simulated.
128 devices in a mesh: view: 16 (over x, y), edge: 8 (over z, core).
Axes of the slice: x: 4, y: 4, z: 4, core: 2. Of those that a mesh axis runs over, the one named last changes fastest.
Arguments:
- log_depth: float32 [1024, 12288], P('view', 'edge'), may hold values from -0.6 to 0.6
- depth_m: float32 [1024, 12288], P('view', 'edge'), may hold values from -12 to 12
- depth_v: float32 [1024, 12288], P('view', 'edge'), may hold values from 1 to 100
- pose: float32 [13, 1024], P(None, ('view', 'edge')), may hold values from -1 to 6, as said below
- pose_m: float32 [13, 1024], P(None, ('view', 'edge')), may hold values from -5 to 5
- pose_v: float32 [13, 1024], P(None, ('view', 'edge')), may hold values from 0.1 to 10
- pairs: int32 [2048, 2], replicated, may hold values from 0 to 1023, as said below
- points: bfloat16 [2048, 3, 12288], P(('view', 'edge')), may hold values from -6 to 6
- conf: bfloat16 [2048, 12288], P(('view', 'edge')), may hold values from 1 to 10
Outputs:
- new_depth: float32 [1024, 12288], P('view', 'edge')
- new_depth_m: float32 [1024, 12288], P('view', 'edge')
- new_depth_v: float32 [1024, 12288], P('view', 'edge')
- new_pose: float32 [13, 1024], P(None, ('view', 'edge'))
- new_pose_m: float32 [13, 1024], P(None, ('view', 'edge'))
- new_pose_v: float32 [13, 1024], P(None, ('view', 'edge'))
Inputs may be any that keep to these rules, and one draw needn't show every extreme that they name: `pairs`: row e is edge e; rows d * 16 to (d + 1) * 16 - 1 are the edges of device d of view+edge. Column 0 is the view whose camera frame the pointmap is given in, column 1 the view whose pixels it covers. Among one device's edges at most 2 name a second view in any one block of 64 consecutive views, and exactly 2 do so in at least one block. `pose`: rows 0-8 hold each view's matrix near the identity, rows 9-11 its centre, row 12 a log focal length between log 80 and log 160.
All inputs are finite; a program needn't handle non-finite values.
Results may differ from a plain program's by a relative error of at most 0.0017.
Values may be sent and summed in bfloat16 or wider, within the bound.
No kernel may reach another device: no remote copies, remote signals or barrier semaphores. Data moves between devices by JAX's collectives and lax.ppermute only.
A program may use at most 64 MiB of HBM per device.

v0:
```python
import functools

import jax
import jax.numpy as jnp
from jax import lax
from jax.experimental import pallas as pl
from jax.experimental.pallas import tpu as pltpu
from jax.sharding import PartitionSpec as P

H = 128
W = 96
ITERS = 2
STEPS_DONE = 10
ROWS = 13
LANES = 128
CAP = 2

learn_rate = 0.01
beta_first = 0.9
beta_second = 0.999
adam_eps = 1e-08

f32 = jnp.float32
bf16 = jnp.bfloat16
EXACT = lax.Precision.HIGHEST


def adam(param, moment, second, grad, count):
    moment = beta_first * moment + (1.0 - beta_first) * grad
    second = beta_second * second + (1.0 - beta_second) * grad * grad
    corrected = moment * (learn_rate / (1.0 - beta_first**count))
    spread = second * (1.0 / (1.0 - beta_second**count))
    return (param - corrected / (jnp.sqrt(spread) + adam_eps), moment, second)


def iota(shape, dim):
    return lax.broadcasted_iota(jnp.int32, shape, dim)


def dot(a, b, dims=((1,), (0,)), precision=None):
    return lax.dot_general(a, b, (dims, ((), ())), precision=precision, preferred_element_type=f32)


def fold_matrix():
    return (iota((LANES, LANES), 0) // 8 == iota((LANES, LANES), 1)).astype(f32)


def hot(mask):
    return jnp.where(mask, 1.0, 0.0).astype(bf16)


def make_picker(local):
    rows, edges = local.shape
    hit = (local >= 0) & (local < 64)
    tri = hot(iota((edges, edges), 0) < iota((edges, edges), 1))
    rank = dot(hot(hit), tri)
    slot = (iota((rows, edges), 0) % CAP).astype(f32)
    mine = hit & (rank == slot)
    target = jnp.sum(jnp.where(mine, local + 1, 0).astype(f32), axis=1, keepdims=True)
    return hot((iota((rows, 64), 1) + 1).astype(f32) == target)


def spread_pose(pose_t):
    wide = dot(pose_t, fold_matrix()[:, :ROWS], ((1,), (1,)), EXACT)
    mine = iota(wide.shape, 1) % 8 == iota(wide.shape, 0)
    return jnp.sum(jnp.where(mine, wide, 0.0), axis=0, keepdims=True)


def gather_pose(row):
    wide = jnp.broadcast_to(row, (8, LANES))
    mine = iota(wide.shape, 1) % 8 == iota(wide.shape, 0)
    return dot(jnp.where(mine, wide, 0.0), fold_matrix()[:, :ROWS], ((1,), (0,)), EXACT)


def two_parts(rows):
    lead = rows.astype(bf16).astype(f32)
    even = iota(rows.shape, 0) % 2 == 0
    return jnp.where(even, lead, rows - lead).astype(bf16)


def send_rows(out, picker, depth, pose_row):
    owners, cap, width = out.shape
    pixels = width - LANES
    picked = dot(picker, depth.astype(bf16)).astype(bf16)
    out[:, :, :pixels] = picked.reshape(owners, cap, pixels)
    wide = jnp.broadcast_to(pose_row, (owners * cap, LANES))
    out[:, :, pixels:] = two_parts(wide).reshape(owners, cap, LANES)


def first_kernel(local, depth, pose_t, out, picker_out):
    picker = make_picker(local[...])
    picker_out[...] = picker
    send_rows(out, picker, depth[...], spread_pose(pose_t[...]))


def owner_kernel(count, last, incoming, picker, depth, m, v, pose_t, pose_m, pose_v, *outs):
    owners, cap, width = incoming.shape
    pixels = width - LANES
    grad = dot(picker[...], incoming[:, :, :pixels].reshape(owners * cap, pixels), ((0,), (0,)))
    new = adam(depth[...], m[...], v[...], grad, count)
    for ref, value in zip(outs[:3], new):
        ref[...] = value
    rows = incoming[:, :, pixels:].reshape(owners * cap, LANES)
    pose_grad = jnp.sum(rows.astype(f32), axis=0, keepdims=True) * (1.0 / (pixels * 8))
    state = [spread_pose(ref[...]) for ref in (pose_t, pose_m, pose_v)]
    new_pose = adam(*state, pose_grad, count)
    for ref, value in zip(outs[3:6], new_pose):
        ref[...] = gather_pose(value)
    if not last:
        send_rows(outs[6], picker[...], new[0], new_pose[0])


def edge_kernel(arrived, mine, mine_t, points, conf, out, depth_s, grad_s):
    groups, shards, cap, width = arrived.shape
    pixels = width - LANES
    edges = mine.shape[0]
    owners = groups * shards
    group = mine[:, 1:2] // 64
    group_row = mine_t[1:2, :] // 64
    earlier = iota((edges, edges), 1) < iota((edges, edges), 0)
    slot = jnp.sum(jnp.where((group == group_row) & earlier, 1.0, 0.0), axis=1, keepdims=True)
    sel = hot((group * cap).astype(f32) + slot == iota((edges, groups * cap), 1).astype(f32))

    for s in range(shards):
        rows = arrived[:, s, :, :pixels].reshape(groups * cap, pixels)
        depth_s[:, s * pixels : (s + 1) * pixels] = dot(sel, rows)

    both = jnp.concatenate([mine[:, 0:1], mine[:, 1:2]], axis=0)
    pose_rows = arrived[:, :, :, pixels:].reshape(owners * cap, LANES)
    owner_hot = hot(iota((2 * edges, owners * cap), 1) // cap == both // 8)
    lane_mask = iota((2 * edges, LANES), 1) % 8 == both % 8
    fold = fold_matrix()
    wide = jnp.where(lane_mask, dot(owner_hot, pose_rows), 0.0)
    poses = dot(wide, fold, ((1,), (0,)), EXACT)
    pf = [poses[:edges, k : k + 1] for k in range(12)]
    ps = [poses[edges:, k : k + 1] for k in range(13)]
    inv_f = jnp.exp(-ps[12])
    shift = [ps[9 + b] - pf[9 + b] for b in range(3)]
    mix = [[sum(pf[3 * b + a] * ps[3 * b + c] for b in range(3)) for c in range(3)] for a in range(3)]
    base = [sum(pf[3 * b + a] * shift[b] for b in range(3)) for a in range(3)]
    alpha = [mix[a][0] * inv_f for a in range(3)]
    beta = [mix[a][1] * inv_f for a in range(3)]
    tile = (edges, LANES)
    wide_alpha = [jnp.broadcast_to(x, tile) for x in alpha]
    wide_beta = [jnp.broadcast_to(x, tile) for x in beta]
    wide_gamma = [jnp.broadcast_to(mix[a][2], tile) for a in range(3)]
    wide_base = [jnp.broadcast_to(x, tile) for x in base]

    period = 3 * LANES
    lines = period // W
    lane = iota((1, LANES), 1)
    us = []
    vs = []
    for k in range(3):
        index = lane + k * LANES
        line = sum((index >= W * (j + 1)).astype(jnp.int32) for j in range(lines - 1))
        us.append((index - line * W).astype(f32) - (W - 1) / 2.0)
        vs.append(line.astype(f32) - (H - 1) / 2.0)

    def step(i, sums):
        sums = list(sums)
        for k in range(3):
            at = pl.ds(pl.multiple_of(i * period + k * LANES, LANES), LANES)
            u = us[k]
            v = vs[k] + (i * lines).astype(f32)
            dep = jnp.exp(depth_s[:, at])
            weight = conf[:, at].astype(f32)
            weight = weight + weight
            grad = None
            for a in range(3):
                q = wide_alpha[a] * u + (wide_beta[a] * v + wide_gamma[a])
                r = weight * (dep * q + (wide_base[a] - points[a, :, at].astype(f32)))
                t = r * dep
                grad = t * q if grad is None else grad + t * q
                sums[a] = sums[a] + r
                sums[3 + a] = sums[3 + a] + t * u
                sums[6 + a] = sums[6 + a] + t * v
                sums[9 + a] = sums[9 + a] + t
            grad_s[:, at] = grad.astype(bf16)
        return tuple(sums)

    zero = jnp.zeros(tile, f32)
    sums = lax.fori_loop(0, shards * pixels // period, step, (zero,) * 12)
    sums = [jnp.sum(x, axis=1, keepdims=True) for x in sums]

    for s in range(shards):
        placed = dot(sel, grad_s[:, s * pixels : (s + 1) * pixels], ((0,), (0,))).astype(bf16)
        out[:, s, :, :pixels] = placed.reshape(groups, cap, pixels)

    s_sum, u_sum, v_sum, d_sum = sums[:3], sums[3:6], sums[6:9], sums[9:]
    moments = [[u_sum[a] * inv_f, v_sum[a] * inv_f, d_sum[a]] for a in range(3)]
    grad_first = [None] * 13
    grad_second = [None] * 13
    for b in range(3):
        for a in range(3):
            grad_first[3 * b + a] = sum(ps[3 * b + c] * moments[a][c] for c in range(3)) + shift[b] * s_sum[a]
        for c in range(3):
            grad_second[3 * b + c] = sum(pf[3 * b + a] * moments[a][c] for a in range(3))
        grad_second[9 + b] = sum(pf[3 * b + a] * s_sum[a] for a in range(3))
        grad_first[9 + b] = -grad_second[9 + b]
    grad_second[12] = -sum(alpha[a] * u_sum[a] + beta[a] * v_sum[a] for a in range(3))
    lanes = iota(tile, 1)
    tables = []
    for grads in (grad_first, grad_second):
        table = jnp.zeros(tile, f32)
        for k, g in enumerate(grads):
            if g is not None:
                table = jnp.where(lanes == k, g, table)
        tables.append(table)
    table = jnp.concatenate(tables, axis=0)
    expanded = jnp.where(lane_mask, dot(table, fold, ((1,), (1,)), EXACT), 0.0)
    owned = dot(owner_hot.astype(f32), expanded, ((0,), (0,)), EXACT)
    out[:, :, :, pixels:] = two_parts(owned).reshape(groups, shards, cap, LANES)


def call(kernel, outs, scratch=()):
    return pl.pallas_call(
        kernel,
        out_shape=outs,
        scratch_shapes=list(scratch),
        compiler_params=pltpu.CompilerParams(vmem_limit_bytes=40 * 1024 * 1024),
    )


def shards(log_depth, depth_m, depth_v, pose, pose_m, pose_v, pairs, points, conf):
    n_view = lax.axis_size("view")
    n_edge = lax.axis_size("edge")
    owners = n_view * n_edge
    views, pixels = log_depth.shape
    edges = points.shape[0]
    width = pixels + LANES
    me = lax.axis_index(("view", "edge"))
    seconds = pairs[:, 1].reshape(owners, edges)
    local = jnp.repeat(seconds - lax.axis_index("view") * views, CAP, axis=0)
    mine = lax.dynamic_slice_in_dim(pairs, me * edges, edges, 0)
    planes = points.transpose(1, 0, 2)

    S = jax.ShapeDtypeStruct
    message = S((owners, CAP, width), bf16)
    depth_out = [S((views, pixels), f32)] * 3
    pose_out = [S((8, ROWS), f32)] * 3
    exchange = functools.partial(
        lax.all_to_all, axis_name=("view", "edge"), split_axis=0, concat_axis=0, tiled=True
    )

    poses = [pose.T, pose_m.T, pose_v.T]
    depths = [log_depth, depth_m, depth_v]
    sending, picker = call(first_kernel, [message, S((owners * CAP, views), bf16)])(
        local, log_depth, poses[0]
    )
    for turn in range(ITERS):
        arrived = exchange(sending).reshape(n_view, n_edge, CAP, width)
        back = call(
            edge_kernel,
            S((n_view, n_edge, CAP, width), bf16),
            [pltpu.VMEM((edges, pixels * n_edge), f32), pltpu.VMEM((edges, pixels * n_edge), bf16)],
        )(arrived, mine, mine.T, planes, conf)
        incoming = exchange(back.reshape(owners, CAP, width))
        last = turn == ITERS - 1
        kernel = functools.partial(owner_kernel, STEPS_DONE + turn + 1, last)
        results = call(kernel, depth_out + pose_out + ([] if last else [message]))(
            incoming, picker, *depths, *poses
        )
        depths, poses = results[:3], results[3:6]
        if not last:
            sending = results[6]
    return (*depths, *[p.T for p in poses])


def solution(mesh):
    depth = P("view", "edge")
    pose = P(None, ("view", "edge"))
    in_specs = (depth,) * 3 + (pose,) * 3 + (P(), P(("view", "edge"), None, None), P(("view", "edge"), None))
    out_specs = (depth,) * 3 + (pose,) * 3
    return jax.shard_map(shards, mesh=mesh, in_specs=in_specs, out_specs=out_specs, check_vma=False)
```

profile of v0, /device:TPU:1, one launch (start us, length us, event | category | flops | bytes accessed | tf_op | source)
XLA Modules:
  0.0 109.3 jit_solution(12458432852985556041)
XLA Ops:
  0.6 0.7 subtract_reduce_fusion
  1.4 0.1 sub.11
  1.5 0.0 copy-start
  1.5 0.0 copy-start.1
  1.6 0.0 copy-start.2
  1.6 1.1 %copy-done.2 = f32[64,1536]{1,0:T(8,128)S(1)} copy-done((f32[64,1536]{1,0:T(8,128)S(1)}, f32[64,1536]{1,0:T(8,128)}, u32[]{:S(2)}) %copy-start.2) | copy-done | bytes 393240
  2.7 0.7 copy-done.6
  3.4 1.5 %shard_map.136 = (bf16[128,2,1664]{2,1,0:T(2,128)(2,1)}, bf16[256,64]{1,0:T(8,128)(2,1)S(1)}) custom-call(s32[256,16]{1,0:T(8,128)S(1)} %bitcast.20, f32[64,1536]{1,0:T(8,128)S(1)} %copy-done.2, f32[8,13]{1,0:T(8,128)S(1)} %bitcast.21), custom_call_target="tpu_custom_call" | custom-call | tf_op jit(solution)/shard_map/pallas_call | solution.py:248
  4.9 11.5 %all-to-all-start = ((bf16[128,2,1664]{2,1,0:T(2,128)(2,1)}), bf16[128,2,1664]{2,1,0:T(2,128)(2,1)S(1)}, u32[]{:S(2)}, u32[]{:S(2)}) async-start(bf16[128,2,1664]{2,1,0:T(2,128)(2,1)} %get-tuple-element.21), calls=%async_computation | async-start | bytes 1703936 | tf_op jit(solution)/shard_map/all_to_all | solution.py:252
  16.4 0.8 constant_dynamic-slice_fusion
  17.2 0.1 copy.17.mine
  17.3 0.7 fusion.mine_t
  18.0 15.6 %all-to-all-done = bf16[128,2,1664]{2,1,0:T(2,128)(2,1)S(1)} async-done(((bf16[128,2,1664]{2,1,0:T(2,128)(2,1)}), bf16[128,2,1664]{2,1,0:T(2,128)(2,1)S(1)}, u32[]{:S(2)}, u32[]{:S(2)}) %all-to-all-start) | async-done | bytes 852000 | tf_op jit(solution)/shard_map/all_to_all | solution.py:252
  33.6 3.9 %shard_map.137 = bf16[16,8,2,1664]{3,2,1,0:T(2,128)(2,1)S(1)} custom-call(bf16[16,8,2,1664]{3,2,1,0:T(2,128)(2,1)S(1)} %bitcast.16, s32[16,2]{1,0:T(8,128)S(1)} %copy.17.mine, s32[2,16]{1,0:T(2,128)S(1)} %fusion.mine_t, bf16[3,16,12288]{2,1,0:T(8,128)(2,1)S(1)} %bitcast.14, bf16[16,12288]{1,0:T(8,128)(2,1)S(1)} %copy-done.1), custom_call_target="tpu_custom_call" | custom-call | tf_op jit(solution)/shard_map/pallas_call | solution.py:253
  37.5 0.0 copy-start.3
  37.5 0.0 copy-start.4
  37.5 0.0 copy-start.5
  37.5 0.0 copy-start.7
  37.5 21.5 %all_to_all.20.incoming = bf16[128,2,1664]{2,1,0:T(2,128)(2,1)S(1)} all-to-all(bf16[128,2,1664]{2,1,0:T(2,128)(2,1)S(1)} %bitcast.19), channel_id=1, replica_groups=mesh['view'=16,'edge'=8] {'view','edge'}, dimensions={0} | all-to-all | bytes 1703936 | tf_op jit(solution)/shard_map/all_to_all | solution.py:258
  59.1 1.4 %shard_map.138 = (f32[64,1536]{1,0:T(8,128)S(1)}, f32[64,1536]{1,0:T(8,128)S(1)}, f32[64,1536]{1,0:T(8,128)S(1)}, f32[8,13]{1,0:T(8,128)S(1)}, f32[8,13]{1,0:T(8...) custom-call(bf16[128,2,1664]{2,1,0:T(2,128)(2,1)S(1)} %all_to_all.20.incoming, ...), custom_call_target="tpu_custom_call" | custom-call | tf_op jit(solution)/shard_map/pallas_call | solution.py:261
  60.5 21.5 %all_to_all.21 = bf16[128,2,1664]{2,1,0:T(2,128)(2,1)S(1)} all-to-all(bf16[128,2,1664]{2,1,0:T(2,128)(2,1)S(1)} %get-tuple-element.23), channel_id=1, replica_groups=mesh['view'=16,'edge'=8] {'view','edge'}, dimensions={0} | all-to-all | bytes 1703936 | tf_op jit(solution)/shard_map/all_to_all | solution.py:252
  82.0 3.9 %shard_map.139 = bf16[16,8,2,1664]{3,2,1,0:T(2,128)(2,1)S(1)} custom-call(bf16[16,8,2,1664]{3,2,1,0:T(2,128)(2,1)S(1)} %bitcast.17, s32[16,2]{1,0:T(8,128)S(1)} %copy.17.mine, s32[2,16]{1,0:T(2,128)S(1)} %fusion.mine_t, bf16[3,16,12288]{2,1,0:T(8,128)(2,1)S(1)} %bitcast.15, bf16[16,12288]{1,0:T(8,128)(2,1)S(1)} %copy-done.1), custom_call_target="tpu_custom_call" | custom-call | tf_op jit(solution)/shard_map/pallas_call | solution.py:253
  86.0 21.5 %all_to_all.22.incoming = bf16[128,2,1664]{2,1,0:T(2,128)(2,1)S(1)} all-to-all(bf16[128,2,1664]{2,1,0:T(2,128)(2,1)S(1)} %bitcast.18), channel_id=1, replica_groups=mesh['view'=16,'edge'=8] {'view','edge'}, dimensions={0} | all-to-all | bytes 1703936 | tf_op jit(solution)/shard_map/all_to_all | solution.py:258
  107.5 1.8 %shard_map.140 = (f32[64,1536]{1,0:T(8,128)}, f32[64,1536]{1,0:T(8,128)}, f32[64,1536]{1,0:T(8,128)}, f32[8,13]{1,0:T(8,128)}, f32[8,13]{1,0:T(8,128)}, /*index=5*/f32[8,13]{1,0:T(8,128)}) custom-call(bf16[128,2,1664]{2,1,0:T(2,128)(2,1)S(1)} %all_to_all.22.incoming, bf16[256,64]{1,0:T(8,128)(2,1)S(1)} %get-tuple-element.22.picker, ...), custom_call_target="tpu_custom_call" | custom-call | tf_op jit(solution)/shard_map/pallas_call | solution.py:261
  (12 shorter events, 0.1 us)
Async XLA Ops:
  1.5 32.1 %copy-start = (bf16[16,3,12288]{2,0,1:T(8,128)(2,1)S(1)}, bf16[16,3,12288]{2,0,1:T(8,128)(2,1)}, u32[]{:S(2)}) copy-start(bf16[16,3,12288]{2,0,1:T(8,128)(2,1)} %param.16) | copy-start | bytes 3538948
  1.5 32.0 %copy-start.1 = (bf16[16,12288]{1,0:T(8,128)(2,1)S(1)}, bf16[16,12288]{1,0:T(8,128)(2,1)}, u32[]{:S(2)}) copy-start(bf16[16,12288]{1,0:T(8,128)(2,1)} %conf.3) | copy-start | bytes 1179652
  1.6 1.1 %copy-start.2 = (f32[64,1536]{1,0:T(8,128)S(1)}, f32[64,1536]{1,0:T(8,128)}, u32[]{:S(2)}) copy-start(f32[64,1536]{1,0:T(8,128)} %depth.3) | copy-start | bytes 1179652
  2.7 0.7 copy-start.6
  4.9 28.7 %all-to-all-start = ((bf16[128,2,1664]{2,1,0:T(2,128)(2,1)}), bf16[128,2,1664]{2,1,0:T(2,128)(2,1)S(1)}, u32[]{:S(2)}, u32[]{:S(2)}) async-start(bf16[128,2,1664]{2,1,0:T(2,128)(2,1)} %get-tuple-element.21), calls=%async_computation | async-start | bytes 1703936 | tf_op jit(solution)/shard_map/all_to_all | solution.py:252
  37.5 21.6 %copy-start.3 = (f32[64,1536]{1,0:T(8,128)S(1)}, f32[64,1536]{1,0:T(8,128)}, u32[]{:S(2)}) copy-start(f32[64,1536]{1,0:T(8,128)} %depth.3) | copy-start | bytes 1179652
  37.5 21.6 %copy-start.4 = (f32[64,1536]{1,0:T(8,128)S(1)}, f32[64,1536]{1,0:T(8,128)}, u32[]{:S(2)}) copy-start(f32[64,1536]{1,0:T(8,128)} %m.1) | copy-start | bytes 1179652
  37.5 21.6 %copy-start.5 = (f32[64,1536]{1,0:T(8,128)S(1)}, f32[64,1536]{1,0:T(8,128)}, u32[]{:S(2)}) copy-start(f32[64,1536]{1,0:T(8,128)} %v.1) | copy-start | bytes 1179652
  37.5 21.6 %copy-start.7 = (f32[13,8]{0,1:T(8,128)S(1)}, f32[13,8]{0,1:T(8,128)}, u32[]{:S(2)}) copy-start(f32[13,8]{0,1:T(8,128)} %param.12) | copy-start | bytes 1252
  37.5 21.6 %copy-start.8 = (f32[13,8]{0,1:T(8,128)S(1)}, f32[13,8]{0,1:T(8,128)}, u32[]{:S(2)}) copy-start(f32[13,8]{0,1:T(8,128)} %param.13) | copy-start | bytes 1252
  37.5 21.6 %copy-start.9 = (f32[13,8]{0,1:T(8,128)S(1)}, f32[13,8]{0,1:T(8,128)}, u32[]{:S(2)}) copy-start(f32[13,8]{0,1:T(8,128)} %param.14) | copy-start | bytes 1252
where the time goes:
time: 110 us; the launch traced here: 109 us
  blocking collectives  64.6 us (59%)
  waiting for transfers between devices  15.6 us (14%)
  Pallas kernels  12.5 us (11%)
  starting transfers between devices  11.5 us (10%)
  local copies, waits for them, and re-layouts  3.56 us (3%)
    all_to_all x2, blocking collectives, shards(): incoming = exchange(back.reshape(owners, CAP, width))  43 us
    all_to_all x1, blocking collectives, shards(): arrived = exchange(sending).reshape(n_view, n_edge, CAP, width)  21.5 us
    all_to_all x1, waiting for transfers between devices, shards(): arrived = exchange(sending).reshape(n_view, n_edge, CAP, width)  15.6 us
    all_to_all x1, starting transfers between devices, shards(): arrived = exchange(sending).reshape(n_view, n_edge, CAP, width)  11.5 us
    pallas_call x2, Pallas kernels, shards(): call(edge_kernel, S((n_view, n_edge, CAP, width), bf16), [pltpu.VMEM((edg...  7.77 us
    pallas_call x2, Pallas kernels, shards(): call(kernel, depth_out + pose_out + ([] if last else [message]))  3.21 us
  transfers between devices with their start and end apart: 1, of which 1 were waited for; matrix products, arithmetic and copies ran while one was open for 1% of the time, Pallas kernels for 0%

commit v1 on v0

v1 whole, which is shorter than its diff:
```python
import functools

import jax
import jax.numpy as jnp
from jax import lax
from jax.experimental import pallas as pl
from jax.experimental.pallas import tpu as pltpu
from jax.sharding import PartitionSpec as P

H = 128
W = 96
ITERS = 2
STEPS_DONE = 10
ROWS = 13
LANES = 128
CAP = 2

learn_rate = 0.01
beta_first = 0.9
beta_second = 0.999
adam_eps = 1e-08

f32 = jnp.float32
bf16 = jnp.bfloat16
EXACT = lax.Precision.HIGHEST


def adam(param, moment, second, half, count, scale):
    moment = beta_first * moment + ((1.0 - beta_first) * scale) * half
    second = beta_second * second + ((1.0 - beta_second) * scale * scale) * (half * half)
    corrected = moment * (learn_rate / (1.0 - beta_first**count))
    spread = second * (1.0 / (1.0 - beta_second**count))
    return (param - corrected / (jnp.sqrt(spread) + adam_eps), moment, second)


def iota(shape, dim):
    return lax.broadcasted_iota(jnp.int32, shape, dim)


def dot(a, b, dims=((1,), (0,)), precision=None):
    return lax.dot_general(a, b, (dims, ((), ())), precision=precision, preferred_element_type=f32)


def fold_matrix():
    return (iota((LANES, LANES), 0) // 8 == iota((LANES, LANES), 1)).astype(f32)


def hot(mask):
    return jnp.where(mask, 1.0, 0.0).astype(bf16)


def make_picker(seconds, start, views):
    lines = seconds.shape[0]
    slots = lines * 8 * CAP
    local = seconds - start
    value = jnp.where((local >= 0) & (local < views), local + 1, 0).astype(f32).astype(bf16)
    row = iota((slots, LANES), 0)
    lane = iota((slots, LANES), 1)
    spread = dot(hot(iota((slots, lines), 0) // (8 * CAP) == iota((slots, lines), 1)), value)
    hit = (spread > 0.5) & (lane // 16 == (row // CAP) % 8)
    tri = hot(iota((LANES, LANES), 0) < iota((LANES, LANES), 1))
    rank = dot(hot(hit), tri)
    mine = hit & (rank == (row % CAP).astype(f32))
    target = jnp.sum(jnp.where(mine, spread, 0.0), axis=1, keepdims=True)
    return hot((iota((slots, views), 1) + 1).astype(f32) == target)


def spread_pose(pose_t):
    lane = iota((8, LANES), 1)
    wide = jnp.zeros((8, LANES), f32)
    for k in range(ROWS):
        wide = jnp.where(lane == iota((8, LANES), 0) + 8 * k, pose_t[:, k : k + 1], wide)
    return jnp.sum(wide, axis=0, keepdims=True)


def gather_pose(row):
    wide = jnp.broadcast_to(row, (8, LANES))
    mine = iota(wide.shape, 1) % 8 == iota(wide.shape, 0)
    return dot(jnp.where(mine, wide, 0.0), fold_matrix()[:, :ROWS], ((1,), (0,)), EXACT)


def two_parts(rows):
    lead = rows.astype(bf16).astype(f32)
    even = iota(rows.shape, 0) % 2 == 0
    return jnp.where(even, lead, rows - lead).astype(bf16)


def send_rows(out, picker, depth, pose_row):
    owners, cap, width = out.shape
    pixels = width - LANES
    picked = dot(picker, depth.astype(bf16)).astype(bf16)
    out[:, :, :pixels] = picked.reshape(owners, cap, pixels)
    wide = jnp.broadcast_to(pose_row, (owners * cap, LANES))
    out[:, :, pixels:] = two_parts(wide).reshape(owners, cap, LANES)


def first_kernel(pairs_hbm, depth_hbm, pose_hbm, out, picker_out, mine, mine_t, pairs, depth, pose_t, sems):
    sources = (pairs_hbm, pose_hbm, depth_hbm)
    copies = [
        pltpu.make_async_copy(src, dst, sems.at[k])
        for k, (src, dst) in enumerate(zip(sources, (pairs, pose_t, depth)))
    ]
    for copy in copies:
        copy.start()
    copies[0].wait()
    views = depth.shape[0]
    picker = make_picker(pairs[:, 1, :], lax.axis_index("view") * views, views)
    picker_out[...] = picker
    copies[1].wait()
    row = spread_pose(pose_t[...])
    copies[2].wait()
    send_rows(out, picker, depth[...], row)

    edges = mine.shape[0]
    me = lax.axis_index("view") * lax.axis_size("edge") + lax.axis_index("edge")
    line = pairs[me // (LANES // edges)].astype(f32)
    lanes = iota((edges, LANES), 1)
    pick = (lanes == me % (LANES // edges) * edges + iota((edges, LANES), 0)).astype(f32)
    for ref, value in (
        (mine, dot(pick, line, ((1,), (1,)), EXACT)),
        (mine_t, dot(line, pick, ((1,), (1,)), EXACT)),
    ):
        ref[...] = (value + 0.5).astype(jnp.int32)


def owner_kernel(count, last, incoming, picker, depth, m, v, pose_t, pose_m, pose_v, *outs):
    owners, cap, width = incoming.shape
    pixels = width - LANES
    grad = dot(picker[...], incoming[:, :, :pixels].reshape(owners * cap, pixels), ((0,), (0,)))
    new = adam(depth[...], m[...], v[...], grad, count, 2.0)
    for ref, value in zip(outs[:3], new):
        ref[...] = value
    rows = incoming[:, :, pixels:].reshape(owners * cap, LANES)
    pose_grad = jnp.sum(rows.astype(f32), axis=0, keepdims=True)
    state = [ref[...] if last else spread_pose(ref[...]) for ref in (pose_t, pose_m, pose_v)]
    new_pose = adam(*state, pose_grad, count, 2.0 / (H * W))
    for ref, value in zip(outs[3:6], new_pose):
        ref[...] = gather_pose(value) if last else value
    if not last:
        send_rows(outs[6], picker[...], new[0], new_pose[0])


def edge_kernel(arrived, mine, mine_t, points, conf, out, depth_s, grad_s):
    groups, shards, cap, width = arrived.shape
    pixels = width - LANES
    edges = mine.shape[0]
    slots = groups * shards * cap

    both = jnp.concatenate([mine[:, 0:1], mine[:, 1:2]], axis=0)
    pose_rows = arrived[:, :, :, pixels:].reshape(slots, LANES)
    slot_of = iota((2 * edges, slots), 1)
    lane_mask = iota((2 * edges, LANES), 1) % 8 == both % 8
    fold = hot(iota((LANES, LANES), 0) // 8 == iota((LANES, LANES), 1))
    poses = None
    for part in range(cap):
        picked = dot(hot(slot_of == both // 8 * cap + part), pose_rows)
        part_poses = dot(jnp.where(lane_mask, picked, 0.0).astype(bf16), fold)
        poses = part_poses if poses is None else poses + part_poses

    group = mine[:, 1:2] // 64
    group_row = mine_t[1:2, :] // 64
    earlier = iota((edges, edges), 1) < iota((edges, edges), 0)
    slot = jnp.sum(jnp.where((group == group_row) & earlier, 1.0, 0.0), axis=1, keepdims=True)
    sel = hot((group * cap).astype(f32) + slot == iota((edges, groups * cap), 1).astype(f32))
    for s in range(shards):
        rows = arrived[:, s, :, :pixels].reshape(groups * cap, pixels)
        depth_s[:, s * pixels : (s + 1) * pixels] = dot(sel, rows)

    pf = [poses[:edges, k : k + 1] for k in range(12)]
    ps = [poses[edges:, k : k + 1] for k in range(13)]
    inv_f = jnp.exp(-ps[12])
    shift = [ps[9 + b] - pf[9 + b] for b in range(3)]
    mix = [[sum(pf[3 * b + a] * ps[3 * b + c] for b in range(3)) for c in range(3)] for a in range(3)]
    base = [sum(pf[3 * b + a] * shift[b] for b in range(3)) for a in range(3)]
    alpha = [mix[a][0] * inv_f for a in range(3)]
    beta = [mix[a][1] * inv_f for a in range(3)]
    tile = (edges, LANES)
    wide_base = [jnp.broadcast_to(x, tile) for x in base]

    period = 3 * LANES
    lines = period // W
    lane = iota((1, LANES), 1)
    us = []
    vs = []
    for k in range(3):
        index = lane + k * LANES
        line = sum((index >= W * (j + 1)).astype(jnp.int32) for j in range(lines - 1))
        us.append((index - line * W).astype(f32) - (W - 1) / 2.0)
        vs.append(line.astype(f32) - (H - 1) / 2.0)
    start = [[alpha[a] * us[k] + (beta[a] * vs[k] + mix[a][2]) for a in range(3)] for k in range(3)]
    slope = [jnp.broadcast_to(beta[a] * float(lines), tile) for a in range(3)]

    def step(i, sums):
        s_acc, d_acc, e_acc = list(sums[:3]), list(sums[3:12]), list(sums[12:])
        rise = [slope[a] * i.astype(f32) for a in range(3)]
        for k in range(3):
            at = pl.ds(pl.multiple_of(i * period + k * LANES, LANES), LANES)
            dep = jnp.exp(depth_s[:, at])
            weight = conf[:, at].astype(f32)
            grad = None
            for a in range(3):
                q = start[k][a] + rise[a]
                r = weight * (dep * q + (wide_base[a] - points[a, :, at].astype(f32)))
                t = r * dep
                grad = t * q if grad is None else grad + t * q
                s_acc[a] = s_acc[a] + r
                d_acc[3 * k + a] = d_acc[3 * k + a] + t
            grad_s[:, at] = grad.astype(bf16)
        for a in range(3):
            e_acc[a] = e_acc[a] + ((d_acc[a] + d_acc[3 + a]) + d_acc[6 + a])
        return (*s_acc, *d_acc, *e_acc)

    steps = shards * pixels // period
    sums = lax.fori_loop(0, steps, step, (jnp.zeros(tile, f32),) * 15)

    def total(x):
        return jnp.sum(x, axis=1, keepdims=True)

    d_acc = sums[3:12]
    d_all = [(d_acc[a] + d_acc[3 + a]) + d_acc[6 + a] for a in range(3)]
    s_sum = [total(x) for x in sums[:3]]
    d_sum = [total(x) for x in d_all]
    u_sum = [total(sum(d_acc[3 * k + a] * us[k] for k in range(3))) for a in range(3)]
    v_sum = [
        total(
            sum(d_acc[3 * k + a] * vs[k] for k in range(3))
            + float(lines) * (float(steps) * d_all[a] - sums[12 + a])
        )
        for a in range(3)
    ]

    for s in range(shards):
        placed = dot(sel, grad_s[:, s * pixels : (s + 1) * pixels], ((0,), (0,))).astype(bf16)
        out[:, s, :, :pixels] = placed.reshape(groups, cap, pixels)

    moments = [[u_sum[a] * inv_f, v_sum[a] * inv_f, d_sum[a]] for a in range(3)]
    grad_first = [None] * 12
    grad_second = [None] * 13
    for b in range(3):
        for a in range(3):
            grad_first[3 * b + a] = sum(ps[3 * b + c] * moments[a][c] for c in range(3)) + shift[b] * s_sum[a]
        for c in range(3):
            grad_second[3 * b + c] = sum(pf[3 * b + a] * moments[a][c] for a in range(3))
        grad_second[9 + b] = sum(pf[3 * b + a] * s_sum[a] for a in range(3))
        grad_first[9 + b] = -grad_second[9 + b]
    grad_second[12] = -sum(alpha[a] * u_sum[a] + beta[a] * v_sum[a] for a in range(3))
    component = iota(tile, 1) // 8
    tables = []
    for grads in (grad_first, grad_second):
        table = jnp.zeros(tile, f32)
        for k, g in enumerate(grads):
            table = jnp.where(component == k, g, table)
        tables.append(table)
    table = jnp.where(lane_mask, jnp.concatenate(tables, axis=0), 0.0)
    lead = table.astype(bf16)
    rest = (table - lead.astype(f32)).astype(bf16)
    both_row = jnp.concatenate([mine_t[0:1, :], mine_t[1:2, :]], axis=1)
    owner_hot = hot(iota((slots, 2 * edges), 0) // cap == both_row // 8)
    owned = dot(owner_hot, lead) + dot(owner_hot, rest)
    out[:, :, :, pixels:] = two_parts(owned).reshape(groups, shards, cap, LANES)


def call(kernel, outs, scratch=(), in_specs=None, mib=40):
    extra = {} if in_specs is None else {"in_specs": in_specs}
    return pl.pallas_call(
        kernel,
        out_shape=outs,
        scratch_shapes=list(scratch),
        compiler_params=pltpu.CompilerParams(vmem_limit_bytes=mib * 1024 * 1024),
        **extra,
    )


def shards(log_depth, depth_m, depth_v, pose, pose_m, pose_v, pairs, points, conf):
    n_view = lax.axis_size("view")
    n_edge = lax.axis_size("edge")
    owners = n_view * n_edge
    views, pixels = log_depth.shape
    edges = points.shape[0]
    width = pixels + LANES

    S = jax.ShapeDtypeStruct
    message = S((owners, CAP, width), bf16)
    depth_out = [S((views, pixels), f32)] * 3
    exchange = functools.partial(
        lax.all_to_all, axis_name=("view", "edge"), split_axis=0, concat_axis=0, tiled=True
    )

    poses = [pose.T, pose_m.T, pose_v.T]
    depths = [log_depth, depth_m, depth_v]
    hbm = pl.BlockSpec(memory_space=pltpu.HBM)
    sending, picker, mine, mine_t = call(
        first_kernel,
        [message, S((owners * CAP, views), bf16), S((edges, 2), jnp.int32), S((2, edges), jnp.int32)],
        [
            pltpu.VMEM((pairs.shape[0] // LANES, 2, LANES), jnp.int32),
            pltpu.VMEM((views, pixels), f32),
            pltpu.VMEM((8, ROWS), f32),
            pltpu.SemaphoreType.DMA((3,)),
        ],
        [hbm, hbm, hbm],
        64,
    )(pairs.T.reshape(2, -1, LANES).transpose(1, 0, 2), log_depth, poses[0])
    planes = points.transpose(1, 0, 2)
    for turn in range(ITERS):
        arrived = exchange(sending).reshape(n_view, n_edge, CAP, width)
        back = call(
            edge_kernel,
            S((n_view, n_edge, CAP, width), bf16),
            [
                pltpu.VMEM((edges, pixels * n_edge), f32),
                pltpu.VMEM((edges, pixels * n_edge), bf16),
            ],
        )(arrived, mine, mine_t, planes, conf)
        incoming = exchange(back.reshape(owners, CAP, width))
        last = turn == ITERS - 1
        kernel = functools.partial(owner_kernel, STEPS_DONE + turn + 1, last)
        pose_out = [S((8, ROWS) if last else (1, LANES), f32)] * 3
        results = call(kernel, depth_out + pose_out + ([] if last else [message]))(
            incoming, picker, *depths, *poses
        )
        depths, poses = results[:3], results[3:6]
        if not last:
            sending = results[6]
    return (*depths, *[p.T for p in poses])


def solution(mesh):
    depth = P("view", "edge")
    pose = P(None, ("view", "edge"))
    in_specs = (depth,) * 3 + (pose,) * 3 + (P(), P(("view", "edge"), None, None), P(("view", "edge"), None))
    out_specs = (depth,) * 3 + (pose,) * 3
    return jax.shard_map(shards, mesh=mesh, in_specs=in_specs, out_specs=out_specs, check_vma=False)
```

time: 110 us -> 105 us (0.955)
  blocking collectives: 64.6 us -> 93.2 us
  waiting for transfers between devices: 15.6 us -> 0 us
  starting transfers between devices: 11.5 us -> 0 us
  local copies, waits for them, and re-layouts: 3.56 us -> 0.07 us
  Pallas kernels: 12.5 us -> 10.8 us
    all_to_all x1 -> x2, blocking collectives: 21.5 us -> 50.2 us  [shards(): arrived = exchange(sending).reshape(n_view, n_edge, CAP, width)]
    all_to_all x1 -> x0, waiting for transfers between devices: 15.6 us -> none  [shards(): arrived = exchange(sending).reshape(n_view, n_edge, CAP, width)]
    all_to_all x1 -> x0, starting transfers between devices: 11.5 us -> none  [shards(): arrived = exchange(sending).reshape(n_view, n_edge, CAP, width)]
    pallas_call x2, Pallas kernels: 7.77 us -> 5.9 us  [shards(): call(edge_kernel, S((n_view, n_edge, CAP, width), bf16), [pltpu.VMEM((edg...]
    unnamed x20 -> x22, local copies, waits for them, and re-layouts: 1.84 us -> 0.07 us
  transfers between devices with their start and end apart: 1 -> 0, of which waited for: 1 -> 0; matrix products, arithmetic and copies ran while one was open for 1% -> 0% of each run, Pallas kernels for 0% -> 0%
where the time goes in v1:
time: 105 us
  blocking collectives  93.2 us (89%)
  Pallas kernels  10.8 us (10%)
    all_to_all x2, blocking collectives, shards(): arrived = exchange(sending).reshape(n_view, n_edge, CAP, width)  50.2 us
    all_to_all x2, blocking collectives, shards(): incoming = exchange(back.reshape(owners, CAP, width))  43 us
    pallas_call x2, Pallas kernels, shards(): call(edge_kernel, S((n_view, n_edge, CAP, width), bf16), [pltpu.VMEM((edg...  5.9 us
    pallas_call x1, Pallas kernels, shards(): call(first_kernel, [message, S((owners * CAP, views), bf16), S((edges, 2)...  2.55 us
    pallas_call x2, Pallas kernels, shards(): call(kernel, depth_out + pose_out + ([] if last else [message]))  2.38 us

profile of v1, /device:TPU:1, one launch (start us, length us, event | category | flops | bytes accessed | tf_op | source)
XLA Modules:
  0.0 104.9 jit_solution(10046472859855234835)
XLA Ops:
  0.6 2.5 %shard_map.136 = (bf16[128,2,1664]{2,1,0:T(2,128)(2,1)}, bf16[256,64]{1,0:T(8,128)(2,1)}, s32[16,2]{1,0:T(8,128)}, s32[2,16]{1,0:T(2,128)}) custom-call(s32[16,2,128]{2,1,0:T(2,128)} %bitcast.26, f32[64,1536]{1,0:T(8,128)} %depth.1, f32[8,13]{1,0:T(8,128)} %bitcast.22), custom_call_target="tpu_custom_call" | custom-call | tf_op jit(solution)/shard_map/pallas_call | solution.py:292
  3.2 0.0 copy-start
  3.2 0.0 copy-start.1
  3.2 0.0 copy-start.6
  3.2 0.0 copy-start.10
  3.2 28.7 %all_to_all.20 = bf16[128,2,1664]{2,1,0:T(2,128)(2,1)S(1)} all-to-all(bf16[128,2,1664]{2,1,0:T(2,128)(2,1)} %get-tuple-element.23), channel_id=1, replica_groups=mesh['view'=16,'edge'=8] {'view','edge'}, dimensions={0} | all-to-all | bytes 1703936 | tf_op jit(solution)/shard_map/all_to_all | solution.py:306
  31.9 0.0 copy-done
  31.9 0.0 copy-done.1
  31.9 0.0 copy-done.10
  31.9 2.9 %shard_map.137 = bf16[16,8,2,1664]{3,2,1,0:T(2,128)(2,1)S(1)} custom-call(bf16[16,8,2,1664]{3,2,1,0:T(2,128)(2,1)S(1)} %bitcast.20, s32[16,2]{1,0:T(8,128)S(1)} %copy-done.6, s32[2,16]{1,0:T(2,128)S(1)} %copy-done.10, bf16[3,16,12288]{2,1,0:T(8,128)(2,1)S(1)} %bitcast.16, bf16[16,12288]{1,0:T(8,128)(2,1)S(1)} %copy-done.1), custom_call_target="tpu_custom_call" | custom-call | tf_op jit(solution)/shard_map/pallas_call | solution.py:307
  34.9 0.0 copy-start.2
  34.9 0.0 copy-start.3
  34.9 0.0 copy-start.4
  34.9 0.0 copy-start.5
  34.9 0.0 copy-start.7
  35.0 0.0 copy-start.8
  35.0 0.0 copy-start.9
  35.0 21.5 %all_to_all.21.incoming = bf16[128,2,1664]{2,1,0:T(2,128)(2,1)S(1)} all-to-all(bf16[128,2,1664]{2,1,0:T(2,128)(2,1)S(1)} %bitcast.21), channel_id=1, replica_groups=mesh['view'=16,'edge'=8] {'view','edge'}, dimensions={0} | all-to-all | bytes 1703936 | tf_op jit(solution)/shard_map/all_to_all | solution.py:315
  56.5 0.0 copy-done.2
  56.6 0.8 shard_map.138
  57.4 21.5 %all_to_all.22 = bf16[128,2,1664]{2,1,0:T(2,128)(2,1)S(1)} all-to-all(bf16[128,2,1664]{2,1,0:T(2,128)(2,1)S(1)} %get-tuple-element.27), channel_id=1, replica_groups=mesh['view'=16,'edge'=8] {'view','edge'}, dimensions={0} | all-to-all | bytes 1703936 | tf_op jit(solution)/shard_map/all_to_all | solution.py:306
  78.9 3.0 %shard_map.139 = bf16[16,8,2,1664]{3,2,1,0:T(2,128)(2,1)S(1)} custom-call(bf16[16,8,2,1664]{3,2,1,0:T(2,128)(2,1)S(1)} %bitcast.18, s32[16,2]{1,0:T(8,128)S(1)} %copy-done.6, s32[2,16]{1,0:T(2,128)S(1)} %copy-done.10, bf16[3,16,12288]{2,1,0:T(8,128)(2,1)S(1)} %bitcast.17, bf16[16,12288]{1,0:T(8,128)(2,1)S(1)} %copy-done.1), custom_call_target="tpu_custom_call" | custom-call | tf_op jit(solution)/shard_map/pallas_call | solution.py:307
  81.9 21.5 %all_to_all.23.incoming = bf16[128,2,1664]{2,1,0:T(2,128)(2,1)S(1)} all-to-all(bf16[128,2,1664]{2,1,0:T(2,128)(2,1)S(1)} %bitcast.19), channel_id=1, replica_groups=mesh['view'=16,'edge'=8] {'view','edge'}, dimensions={0} | all-to-all | bytes 1703936 | tf_op jit(solution)/shard_map/all_to_all | solution.py:315
  103.4 1.6 %shard_map.140 = (f32[64,1536]{1,0:T(8,128)}, f32[64,1536]{1,0:T(8,128)}, f32[64,1536]{1,0:T(8,128)}, f32[8,13]{1,0:T(8,128)}, f32[8,13]{1,0:T(8,128)}, /*index=5*/f32[8,13]{1,0:T(8,128)}) custom-call(bf16[128,2,1664]{2,1,0:T(2,128)(2,1)S(1)} %all_to_all.23.incoming, bf16[256,64]{1,0:T(8,128)(2,1)S(1)} %copy-done.5, f32[64,1536]{1,0:T(8,128)S(1)} %get-tuple-element.28.depth, ...), custom_call_target="tpu_custom_call" | custom-call | tf_op jit(solution)/shard_map/pallas_call | solution.py:319
  (7 shorter events, 0.0 us)
Async XLA Ops:
  3.2 28.7 %copy-start = (bf16[16,3,12288]{2,0,1:T(8,128)(2,1)S(1)}, bf16[16,3,12288]{2,0,1:T(8,128)(2,1)}, u32[]{:S(2)}) copy-start(bf16[16,3,12288]{2,0,1:T(8,128)(2,1)} %param.16) | copy-start | bytes 3538948
  3.2 28.7 %copy-start.1 = (bf16[16,12288]{1,0:T(8,128)(2,1)S(1)}, bf16[16,12288]{1,0:T(8,128)(2,1)}, u32[]{:S(2)}) copy-start(bf16[16,12288]{1,0:T(8,128)(2,1)} %conf.3) | copy-start | bytes 1179652
  3.2 28.7 %copy-start.6 = (s32[16,2]{1,0:T(8,128)S(1)}, s32[16,2]{1,0:T(8,128)}, u32[]{:S(2)}) copy-start(s32[16,2]{1,0:T(8,128)} %get-tuple-element.24.mine) | copy-start | bytes 388
  3.2 28.7 %copy-start.10 = (s32[2,16]{1,0:T(2,128)S(1)}, s32[2,16]{1,0:T(2,128)}, u32[]{:S(2)}) copy-start(s32[2,16]{1,0:T(2,128)} %get-tuple-element.25.mine_t) | copy-start | bytes 388
  34.9 21.6 %copy-start.2 = (f32[64,1536]{1,0:T(8,128)S(1)}, f32[64,1536]{1,0:T(8,128)}, u32[]{:S(2)}) copy-start(f32[64,1536]{1,0:T(8,128)} %depth.1) | copy-start | bytes 1179652
  34.9 21.6 %copy-start.3 = (f32[64,1536]{1,0:T(8,128)S(1)}, f32[64,1536]{1,0:T(8,128)}, u32[]{:S(2)}) copy-start(f32[64,1536]{1,0:T(8,128)} %m.1) | copy-start | bytes 1179652
  34.9 21.6 %copy-start.4 = (f32[64,1536]{1,0:T(8,128)S(1)}, f32[64,1536]{1,0:T(8,128)}, u32[]{:S(2)}) copy-start(f32[64,1536]{1,0:T(8,128)} %v.1) | copy-start | bytes 1179652
  34.9 21.6 %copy-start.5 = (bf16[256,64]{1,0:T(8,128)(2,1)S(1)}, bf16[256,64]{1,0:T(8,128)(2,1)}, u32[]{:S(2)}) copy-start(bf16[256,64]{1,0:T(8,128)(2,1)} %get-tuple-element.26.picker) | copy-start | bytes 98308
  34.9 21.6 %copy-start.7 = (f32[13,8]{0,1:T(8,128)S(1)}, f32[13,8]{0,1:T(8,128)}, u32[]{:S(2)}) copy-start(f32[13,8]{0,1:T(8,128)} %param.12) | copy-start | bytes 1252
  35.0 21.6 %copy-start.8 = (f32[13,8]{0,1:T(8,128)S(1)}, f32[13,8]{0,1:T(8,128)}, u32[]{:S(2)}) copy-start(f32[13,8]{0,1:T(8,128)} %param.13) | copy-start | bytes 1252
  35.0 21.6 %copy-start.9 = (f32[13,8]{0,1:T(8,128)S(1)}, f32[13,8]{0,1:T(8,128)}, u32[]{:S(2)}) copy-start(f32[13,8]{0,1:T(8,128)} %param.14) | copy-start | bytes 1252

commit v2 on v1

--- a/solution.py
+++ b/solution.py
@@ -94,7 +94,9 @@
     out[:, :, pixels:] = two_parts(wide).reshape(owners, cap, LANES)
 
 
-def first_kernel(pairs_hbm, depth_hbm, pose_hbm, out, picker_out, mine, mine_t, pairs, depth, pose_t, sems):
+def first_kernel(
+    pairs_hbm, depth_hbm, pose_hbm, out_hbm, picker_out, mine, mine_t, pairs, depth, pose_t, out, sems, out_sems
+):
     sources = (pairs_hbm, pose_hbm, depth_hbm)
     copies = [
         pltpu.make_async_copy(src, dst, sems.at[k])
@@ -104,13 +106,6 @@
         copy.start()
     copies[0].wait()
     views = depth.shape[0]
-    picker = make_picker(pairs[:, 1, :], lax.axis_index("view") * views, views)
-    picker_out[...] = picker
-    copies[1].wait()
-    row = spread_pose(pose_t[...])
-    copies[2].wait()
-    send_rows(out, picker, depth[...], row)
-
     edges = mine.shape[0]
     me = lax.axis_index("view") * lax.axis_size("edge") + lax.axis_index("edge")
     line = pairs[me // (LANES // edges)].astype(f32)
@@ -122,22 +117,70 @@
     ):
         ref[...] = (value + 0.5).astype(jnp.int32)
 
-
-def owner_kernel(count, last, incoming, picker, depth, m, v, pose_t, pose_m, pose_v, *outs):
+    picker = make_picker(pairs[:, 1, :], lax.axis_index("view") * views, views)
+    picker_out[...] = picker
+    copies[1].wait()
+    owners, cap, width = out.shape
+    pixels = width - LANES
+    wide = jnp.broadcast_to(spread_pose(pose_t[...]), (owners * cap, LANES))
+    out[:, :, pixels:] = two_parts(wide).reshape(owners, cap, LANES)
+    copies[2].wait()
+    rounded = depth[...].astype(bf16)
+    pieces = out_sems.shape[0]
+    step = owners // pieces
+    sends = []
+    for n in range(pieces):
+        part = pl.ds(n * step, step)
+        picked = dot(picker[n * step * cap : (n + 1) * step * cap], rounded).astype(bf16)
+        out[part, :, :pixels] = picked.reshape(step, cap, pixels)
+        sends.append(pltpu.make_async_copy(out.at[part], out_hbm.at[part], out_sems.at[n]))
+        sends[-1].start()
+    for send in sends:
+        send.wait()
+
+
+def depth_grad(incoming, picker):
     owners, cap, width = incoming.shape
     pixels = width - LANES
-    grad = dot(picker[...], incoming[:, :, :pixels].reshape(owners * cap, pixels), ((0,), (0,)))
-    new = adam(depth[...], m[...], v[...], grad, count, 2.0)
+    return dot(picker[...], incoming[:, :, :pixels].reshape(owners * cap, pixels), ((0,), (0,)))
+
+
+def pose_update(incoming, state, count):
+    owners, cap, width = incoming.shape
+    rows = incoming[:, :, width - LANES :].reshape(owners * cap, LANES)
+    grad = jnp.sum(rows.astype(f32), axis=0, keepdims=True)
+    return adam(*state, grad, count, 2.0 / (H * W))
+
+
+def owner_kernel(count, incoming, picker, depth, m, v, pose_t, pose_m, pose_v, *outs):
+    new = adam(depth[...], m[...], v[...], depth_grad(incoming, picker), count, 2.0)
     for ref, value in zip(outs[:3], new):
         ref[...] = value
-    rows = incoming[:, :, pixels:].reshape(owners * cap, LANES)
-    pose_grad = jnp.sum(rows.astype(f32), axis=0, keepdims=True)
-    state = [ref[...] if last else spread_pose(ref[...]) for ref in (pose_t, pose_m, pose_v)]
-    new_pose = adam(*state, pose_grad, count, 2.0 / (H * W))
+    new_pose = pose_update(incoming, [spread_pose(ref[...]) for ref in (pose_t, pose_m, pose_v)], count)
     for ref, value in zip(outs[3:6], new_pose):
-        ref[...] = gather_pose(value) if last else value
-    if not last:
-        send_rows(outs[6], picker[...], new[0], new_pose[0])
+        ref[...] = value
+    send_rows(outs[6], picker[...], new[0], new_pose[0])
+
+
+def last_kernel(count, incoming, picker, depth, m, v, pose, pose_m, pose_v, *refs):
+    targets, pose_outs, parts, grad_s, sems = refs[:3], refs[3:6], refs[6:9], refs[9], refs[10]
+    grad_s[...] = depth_grad(incoming, picker)
+    pieces = sems.shape[1]
+    step = depth.shape[0] // pieces
+    sends = []
+    for n in range(pieces):
+        rows = pl.ds(n * step, step)
+        new = adam(depth[rows, :], m[rows, :], v[rows, :], grad_s[rows, :], count, 2.0)
+        for k, value in enumerate(new):
+            parts[k][rows, :] = value
+            send = pltpu.make_async_copy(parts[k].at[rows, :], targets[k].at[rows, :], sems.at[k, n])
+            send.start()
+            sends.append(send)
+    new_pose = pose_update(incoming, [ref[...] for ref in (pose, pose_m, pose_v)], count)
+    for ref, value in zip(pose_outs, new_pose):
+        ref[...] = gather_pose(value)
+    for send in sends:
+        send.wait()
 
 
 def edge_kernel(arrived, mine, mine_t, points, conf, out, depth_s, grad_s):
@@ -164,7 +207,7 @@
     sel = hot((group * cap).astype(f32) + slot == iota((edges, groups * cap), 1).astype(f32))
     for s in range(shards):
         rows = arrived[:, s, :, :pixels].reshape(groups * cap, pixels)
-        depth_s[:, s * pixels : (s + 1) * pixels] = dot(sel, rows)
+        depth_s[:, s * pixels : (s + 1) * pixels] = jnp.exp(dot(sel, rows))
 
     pf = [poses[:edges, k : k + 1] for k in range(12)]
     ps = [poses[edges:, k : k + 1] for k in range(13)]
@@ -195,7 +238,7 @@
         rise = [slope[a] * i.astype(f32) for a in range(3)]
         for k in range(3):
             at = pl.ds(pl.multiple_of(i * period + k * LANES, LANES), LANES)
-            dep = jnp.exp(depth_s[:, at])
+            dep = depth_s[:, at]
             weight = conf[:, at].astype(f32)
             grad = None
             for a in range(3):
@@ -211,7 +254,7 @@
         return (*s_acc, *d_acc, *e_acc)
 
     steps = shards * pixels // period
-    sums = lax.fori_loop(0, steps, step, (jnp.zeros(tile, f32),) * 15)
+    sums = lax.fori_loop(0, steps, step, (jnp.zeros(tile, f32),) * 15, unroll=4)
 
     def total(x):
         return jnp.sum(x, axis=1, keepdims=True)
@@ -260,8 +303,10 @@
     out[:, :, :, pixels:] = two_parts(owned).reshape(groups, shards, cap, LANES)
 
 
-def call(kernel, outs, scratch=(), in_specs=None, mib=40):
+def call(kernel, outs, scratch=(), in_specs=None, mib=40, out_specs=None):
     extra = {} if in_specs is None else {"in_specs": in_specs}
+    if out_specs is not None:
+        extra["out_specs"] = out_specs
     return pl.pallas_call(
         kernel,
         out_shape=outs,
@@ -289,6 +334,7 @@
     poses = [pose.T, pose_m.T, pose_v.T]
     depths = [log_depth, depth_m, depth_v]
     hbm = pl.BlockSpec(memory_space=pltpu.HBM)
+    vmem = pl.BlockSpec(memory_space=pltpu.VMEM)
     sending, picker, mine, mine_t = call(
         first_kernel,
         [message, S((owners * CAP, views), bf16), S((edges, 2), jnp.int32), S((2, edges), jnp.int32)],
@@ -296,10 +342,13 @@
             pltpu.VMEM((pairs.shape[0] // LANES, 2, LANES), jnp.int32),
             pltpu.VMEM((views, pixels), f32),
             pltpu.VMEM((8, ROWS), f32),
+            pltpu.VMEM((owners, CAP, width), bf16),
             pltpu.SemaphoreType.DMA((3,)),
+            pltpu.SemaphoreType.DMA((4,)),
         ],
         [hbm, hbm, hbm],
         64,
+        [hbm, vmem, vmem, vmem],
     )(pairs.T.reshape(2, -1, LANES).transpose(1, 0, 2), log_depth, poses[0])
     planes = points.transpose(1, 0, 2)
     for turn in range(ITERS):
@@ -313,15 +362,21 @@
             ],
         )(arrived, mine, mine_t, planes, conf)
         incoming = exchange(back.reshape(owners, CAP, width))
-        last = turn == ITERS - 1
-        kernel = functools.partial(owner_kernel, STEPS_DONE + turn + 1, last)
-        pose_out = [S((8, ROWS) if last else (1, LANES), f32)] * 3
-        results = call(kernel, depth_out + pose_out + ([] if last else [message]))(
-            incoming, picker, *depths, *poses
-        )
+        count = STEPS_DONE + turn + 1
+        if turn < ITERS - 1:
+            results = call(
+                functools.partial(owner_kernel, count),
+                depth_out + [S((1, LANES), f32)] * 3 + [message],
+            )(incoming, picker, *depths, *poses)
+            sending = results[6]
+        else:
+            results = call(
+                functools.partial(last_kernel, count),
+                depth_out + [S((8, ROWS), f32)] * 3,
+                [pltpu.VMEM((views, pixels), f32)] * 4 + [pltpu.SemaphoreType.DMA((3, 4))],
+                out_specs=[hbm] * 3 + [vmem] * 3,
+            )(incoming, picker, *depths, *poses)
         depths, poses = results[:3], results[3:6]
-        if not last:
-            sending = results[6]
     return (*depths, *[p.T for p in poses])
 
 

time: 105 us -> 106 us (level)
  no operation moved by 1% of the time
where the time goes in v2:
time: 106 us; the launch traced here: 105 us
  blocking collectives  93.2 us (88%)
  Pallas kernels  11.1 us (10%)
    all_to_all x2, blocking collectives, shards(): arrived = exchange(sending).reshape(n_view, n_edge, CAP, width)  50.2 us
    all_to_all x2, blocking collectives, shards(): incoming = exchange(back.reshape(owners, CAP, width))  43 us
    pallas_call x2, Pallas kernels, shards(): call(edge_kernel, S((n_view, n_edge, CAP, width), bf16), [pltpu.VMEM((edg...  4.95 us
    pallas_call x1, Pallas kernels, shards(): call(first_kernel, [message, S((owners * CAP, views), bf16), S((edges, 2)...  3.1 us
    pallas_call x1, Pallas kernels, shards(): call(functools.partial(last_kernel, count), depth_out + [S((8, ROWS), f32...  2.26 us

profile of v2, /device:TPU:1, one launch (start us, length us, event | category | flops | bytes accessed | tf_op | source)
XLA Modules:
  0.0 105.2 jit_solution(8906192320335299685)
XLA Ops:
  0.6 3.1 %shard_map.136 = (bf16[128,2,1664]{2,1,0:T(2,128)(2,1)}, bf16[256,64]{1,0:T(8,128)(2,1)}, s32[16,2]{1,0:T(8,128)}, s32[2,16]{1,0:T(2,128)}) custom-call(s32[16,2,128]{2,1,0:T(2,128)} %bitcast.26, f32[64,1536]{1,0:T(8,128)} %depth.1, f32[8,13]{1,0:T(8,128)} %bitcast.22), custom_call_target="tpu_custom_call" | custom-call | tf_op jit(solution)/shard_map/pallas_call | solution.py:338
  3.7 0.0 copy-start
  3.7 0.0 copy-start.1
  3.8 0.0 copy-start.6
  3.8 0.0 copy-start.10
  3.8 28.7 %all_to_all.20 = bf16[128,2,1664]{2,1,0:T(2,128)(2,1)S(1)} all-to-all(bf16[128,2,1664]{2,1,0:T(2,128)(2,1)} %get-tuple-element.23), channel_id=1, replica_groups=mesh['view'=16,'edge'=8] {'view','edge'}, dimensions={0} | all-to-all | bytes 1703936 | tf_op jit(solution)/shard_map/all_to_all | solution.py:355
  32.5 0.0 copy-done
  32.5 0.0 copy-done.1
  32.5 0.0 copy-done.6
  32.5 2.5 %shard_map.137 = bf16[16,8,2,1664]{3,2,1,0:T(2,128)(2,1)S(1)} custom-call(bf16[16,8,2,1664]{3,2,1,0:T(2,128)(2,1)S(1)} %bitcast.20, s32[16,2]{1,0:T(8,128)S(1)} %copy-done.6, s32[2,16]{1,0:T(2,128)S(1)} %copy-done.10, bf16[3,16,12288]{2,1,0:T(8,128)(2,1)S(1)} %bitcast.16, bf16[16,12288]{1,0:T(8,128)(2,1)S(1)} %copy-done.1), custom_call_target="tpu_custom_call" | custom-call | tf_op jit(solution)/shard_map/pallas_call | solution.py:356
  35.0 0.0 copy-start.2
  35.0 0.0 copy-start.3
  35.0 0.0 copy-start.4
  35.0 0.0 copy-start.5
  35.0 0.0 copy-start.7
  35.0 0.0 copy-start.8
  35.0 0.0 copy-start.9
  35.0 21.5 %all_to_all.21.incoming = bf16[128,2,1664]{2,1,0:T(2,128)(2,1)S(1)} all-to-all(bf16[128,2,1664]{2,1,0:T(2,128)(2,1)S(1)} %bitcast.21), channel_id=1, replica_groups=mesh['view'=16,'edge'=8] {'view','edge'}, dimensions={0} | all-to-all | bytes 1703936 | tf_op jit(solution)/shard_map/all_to_all | solution.py:364
  56.6 0.0 copy-done.3
  56.6 0.8 shard_map.138
  57.5 21.5 %all_to_all.22 = bf16[128,2,1664]{2,1,0:T(2,128)(2,1)S(1)} all-to-all(bf16[128,2,1664]{2,1,0:T(2,128)(2,1)S(1)} %get-tuple-element.27), channel_id=1, replica_groups=mesh['view'=16,'edge'=8] {'view','edge'}, dimensions={0} | all-to-all | bytes 1703936 | tf_op jit(solution)/shard_map/all_to_all | solution.py:355
  79.0 2.5 %shard_map.139 = bf16[16,8,2,1664]{3,2,1,0:T(2,128)(2,1)S(1)} custom-call(bf16[16,8,2,1664]{3,2,1,0:T(2,128)(2,1)S(1)} %bitcast.18, s32[16,2]{1,0:T(8,128)S(1)} %copy-done.6, s32[2,16]{1,0:T(2,128)S(1)} %copy-done.10, bf16[3,16,12288]{2,1,0:T(8,128)(2,1)S(1)} %bitcast.17, bf16[16,12288]{1,0:T(8,128)(2,1)S(1)} %copy-done.1), custom_call_target="tpu_custom_call" | custom-call | tf_op jit(solution)/shard_map/pallas_call | solution.py:356
  81.5 21.5 %all_to_all.23.incoming = bf16[128,2,1664]{2,1,0:T(2,128)(2,1)S(1)} all-to-all(bf16[128,2,1664]{2,1,0:T(2,128)(2,1)S(1)} %bitcast.19), channel_id=1, replica_groups=mesh['view'=16,'edge'=8] {'view','edge'}, dimensions={0} | all-to-all | bytes 1703936 | tf_op jit(solution)/shard_map/all_to_all | solution.py:364
  103.0 2.3 %shard_map.140 = (f32[64,1536]{1,0:T(8,128)}, f32[64,1536]{1,0:T(8,128)}, f32[64,1536]{1,0:T(8,128)}, f32[8,13]{1,0:T(8,128)}, f32[8,13]{1,0:T(8,128)}, /*index=5*/f32[8,13]{1,0:T(8,128)}) custom-call(bf16[128,2,1664]{2,1,0:T(2,128)(2,1)S(1)} %all_to_all.23.incoming, bf16[256,64]{1,0:T(8,128)(2,1)S(1)} %copy-done.5, f32[64,1536]{1,0:T(8,128)S(1)} %get-tuple-element.28.depth, ...), custom_call_target="tpu_custom_call" | custom-call | tf_op jit(solution)/shard_map/pallas_call | solution.py:373
  (7 shorter events, 0.0 us)
Async XLA Ops:
  3.7 28.7 %copy-start = (bf16[16,3,12288]{2,0,1:T(8,128)(2,1)S(1)}, bf16[16,3,12288]{2,0,1:T(8,128)(2,1)}, u32[]{:S(2)}) copy-start(bf16[16,3,12288]{2,0,1:T(8,128)(2,1)} %param.16) | copy-start | bytes 3538948
  3.7 28.7 %copy-start.1 = (bf16[16,12288]{1,0:T(8,128)(2,1)S(1)}, bf16[16,12288]{1,0:T(8,128)(2,1)}, u32[]{:S(2)}) copy-start(bf16[16,12288]{1,0:T(8,128)(2,1)} %conf.3) | copy-start | bytes 1179652
  3.8 28.7 %copy-start.6 = (s32[16,2]{1,0:T(8,128)S(1)}, s32[16,2]{1,0:T(8,128)}, u32[]{:S(2)}) copy-start(s32[16,2]{1,0:T(8,128)} %get-tuple-element.24.mine) | copy-start | bytes 388
  3.8 28.7 %copy-start.10 = (s32[2,16]{1,0:T(2,128)S(1)}, s32[2,16]{1,0:T(2,128)}, u32[]{:S(2)}) copy-start(s32[2,16]{1,0:T(2,128)} %get-tuple-element.25.mine_t) | copy-start | bytes 388
  35.0 21.6 %copy-start.2 = (f32[64,1536]{1,0:T(8,128)S(1)}, f32[64,1536]{1,0:T(8,128)}, u32[]{:S(2)}) copy-start(f32[64,1536]{1,0:T(8,128)} %depth.1) | copy-start | bytes 1179652
  35.0 21.6 %copy-start.3 = (f32[64,1536]{1,0:T(8,128)S(1)}, f32[64,1536]{1,0:T(8,128)}, u32[]{:S(2)}) copy-start(f32[64,1536]{1,0:T(8,128)} %m.1) | copy-start | bytes 1179652
  35.0 21.6 %copy-start.4 = (f32[64,1536]{1,0:T(8,128)S(1)}, f32[64,1536]{1,0:T(8,128)}, u32[]{:S(2)}) copy-start(f32[64,1536]{1,0:T(8,128)} %v.1) | copy-start | bytes 1179652
  35.0 21.6 %copy-start.5 = (bf16[256,64]{1,0:T(8,128)(2,1)S(1)}, bf16[256,64]{1,0:T(8,128)(2,1)}, u32[]{:S(2)}) copy-start(bf16[256,64]{1,0:T(8,128)(2,1)} %get-tuple-element.26.picker) | copy-start | bytes 98308
  35.0 21.6 %copy-start.7 = (f32[13,8]{0,1:T(8,128)S(1)}, f32[13,8]{0,1:T(8,128)}, u32[]{:S(2)}) copy-start(f32[13,8]{0,1:T(8,128)} %param.12) | copy-start | bytes 1252
  35.0 21.6 %copy-start.8 = (f32[13,8]{0,1:T(8,128)S(1)}, f32[13,8]{0,1:T(8,128)}, u32[]{:S(2)}) copy-start(f32[13,8]{0,1:T(8,128)} %param.13) | copy-start | bytes 1252
  35.0 21.6 %copy-start.9 = (f32[13,8]{0,1:T(8,128)S(1)}, f32[13,8]{0,1:T(8,128)}, u32[]{:S(2)}) copy-start(f32[13,8]{0,1:T(8,128)} %param.14) | copy-start | bytes 1252

commit v3 on v1

--- a/solution.py
+++ b/solution.py
@@ -56,8 +56,8 @@
     value = jnp.where((local >= 0) & (local < views), local + 1, 0).astype(f32).astype(bf16)
     row = iota((slots, LANES), 0)
     lane = iota((slots, LANES), 1)
-    spread = dot(hot(iota((slots, lines), 0) // (8 * CAP) == iota((slots, lines), 1)), value)
-    hit = (spread > 0.5) & (lane // 16 == (row // CAP) % 8)
+    spread = dot(hot(row[:, :lines] // CAP % lines == lane[:, :lines]), value)
+    hit = (spread > 0.5) & (lane // 16 == row // (CAP * lines))
     tri = hot(iota((LANES, LANES), 0) < iota((LANES, LANES), 1))
     rank = dot(hot(hit), tri)
     mine = hit & (rank == (row % CAP).astype(f32))
@@ -141,10 +141,13 @@
 
 
 def edge_kernel(arrived, mine, mine_t, points, conf, out, depth_s, grad_s):
-    groups, shards, cap, width = arrived.shape
+    shards, groups, cap, width = arrived.shape
     pixels = width - LANES
     edges = mine.shape[0]
-    slots = groups * shards * cap
+    slots = shards * groups * cap
+
+    def place(view):
+        return view // 8 % shards * groups + view // (8 * shards)
 
     both = jnp.concatenate([mine[:, 0:1], mine[:, 1:2]], axis=0)
     pose_rows = arrived[:, :, :, pixels:].reshape(slots, LANES)
@@ -153,7 +156,7 @@
     fold = hot(iota((LANES, LANES), 0) // 8 == iota((LANES, LANES), 1))
     poses = None
     for part in range(cap):
-        picked = dot(hot(slot_of == both // 8 * cap + part), pose_rows)
+        picked = dot(hot(slot_of == place(both) * cap + part), pose_rows)
         part_poses = dot(jnp.where(lane_mask, picked, 0.0).astype(bf16), fold)
         poses = part_poses if poses is None else poses + part_poses
 
@@ -163,8 +166,8 @@
     slot = jnp.sum(jnp.where((group == group_row) & earlier, 1.0, 0.0), axis=1, keepdims=True)
     sel = hot((group * cap).astype(f32) + slot == iota((edges, groups * cap), 1).astype(f32))
     for s in range(shards):
-        rows = arrived[:, s, :, :pixels].reshape(groups * cap, pixels)
-        depth_s[:, s * pixels : (s + 1) * pixels] = dot(sel, rows)
+        rows = arrived[s, :, :, :pixels].reshape(groups * cap, pixels)
+        depth_s[:, s * pixels : (s + 1) * pixels] = jnp.exp(dot(sel, rows))
 
     pf = [poses[:edges, k : k + 1] for k in range(12)]
     ps = [poses[edges:, k : k + 1] for k in range(13)]
@@ -195,7 +198,7 @@
         rise = [slope[a] * i.astype(f32) for a in range(3)]
         for k in range(3):
             at = pl.ds(pl.multiple_of(i * period + k * LANES, LANES), LANES)
-            dep = jnp.exp(depth_s[:, at])
+            dep = depth_s[:, at]
             weight = conf[:, at].astype(f32)
             grad = None
             for a in range(3):
@@ -211,7 +214,7 @@
         return (*s_acc, *d_acc, *e_acc)
 
     steps = shards * pixels // period
-    sums = lax.fori_loop(0, steps, step, (jnp.zeros(tile, f32),) * 15)
+    sums = lax.fori_loop(0, steps, step, (jnp.zeros(tile, f32),) * 15, unroll=4)
 
     def total(x):
         return jnp.sum(x, axis=1, keepdims=True)
@@ -231,7 +234,7 @@
 
     for s in range(shards):
         placed = dot(sel, grad_s[:, s * pixels : (s + 1) * pixels], ((0,), (0,))).astype(bf16)
-        out[:, s, :, :pixels] = placed.reshape(groups, cap, pixels)
+        out[s, :, :, :pixels] = placed.reshape(groups, cap, pixels)
 
     moments = [[u_sum[a] * inv_f, v_sum[a] * inv_f, d_sum[a]] for a in range(3)]
     grad_first = [None] * 12
@@ -255,9 +258,9 @@
     lead = table.astype(bf16)
     rest = (table - lead.astype(f32)).astype(bf16)
     both_row = jnp.concatenate([mine_t[0:1, :], mine_t[1:2, :]], axis=1)
-    owner_hot = hot(iota((slots, 2 * edges), 0) // cap == both_row // 8)
+    owner_hot = hot(iota((slots, 2 * edges), 0) // cap == place(both_row))
     owned = dot(owner_hot, lead) + dot(owner_hot, rest)
-    out[:, :, :, pixels:] = two_parts(owned).reshape(groups, shards, cap, LANES)
+    out[:, :, :, pixels:] = two_parts(owned).reshape(shards, groups, cap, LANES)
 
 
 def call(kernel, outs, scratch=(), in_specs=None, mib=40):
@@ -283,7 +286,7 @@
     message = S((owners, CAP, width), bf16)
     depth_out = [S((views, pixels), f32)] * 3
     exchange = functools.partial(
-        lax.all_to_all, axis_name=("view", "edge"), split_axis=0, concat_axis=0, tiled=True
+        lax.all_to_all, axis_name=("edge", "view"), split_axis=0, concat_axis=0, tiled=True
     )
 
     poses = [pose.T, pose_m.T, pose_v.T]
@@ -303,10 +306,10 @@
     )(pairs.T.reshape(2, -1, LANES).transpose(1, 0, 2), log_depth, poses[0])
     planes = points.transpose(1, 0, 2)
     for turn in range(ITERS):
-        arrived = exchange(sending).reshape(n_view, n_edge, CAP, width)
+        arrived = exchange(sending).reshape(n_edge, n_view, CAP, width)
         back = call(
             edge_kernel,
-            S((n_view, n_edge, CAP, width), bf16),
+            S((n_edge, n_view, CAP, width), bf16),
             [
                 pltpu.VMEM((edges, pixels * n_edge), f32),
                 pltpu.VMEM((edges, pixels * n_edge), bf16),

time: 105 us -> 102 us (0.971)
  blocking collectives: 93.2 us -> 91.2 us
    all_to_all x2, blocking collectives: 50.2 us -> 49.1 us  [shards(): arrived = exchange(sending).reshape(n_edge, n_view, CAP, width)]
where the time goes in v3:
time: 102 us
  blocking collectives  91.2 us (89%)
  Pallas kernels  9.94 us (10%)
    all_to_all x2, blocking collectives, shards(): arrived = exchange(sending).reshape(n_edge, n_view, CAP, width)  49.1 us
    all_to_all x2, blocking collectives, shards(): incoming = exchange(back.reshape(owners, CAP, width))  42.1 us
    pallas_call x2, Pallas kernels, shards(): call(edge_kernel, S((n_edge, n_view, CAP, width), bf16), [pltpu.VMEM((edg...  5 us
    pallas_call x1, Pallas kernels, shards(): call(first_kernel, [message, S((owners * CAP, views), bf16), S((edges, 2)...  2.55 us
    pallas_call x2, Pallas kernels, shards(): call(kernel, depth_out + pose_out + ([] if last else [message]))  2.39 us

profile of v3, /device:TPU:1, one launch (start us, length us, event | category | flops | bytes accessed | tf_op | source)
XLA Modules:
  0.0 102.0 jit_solution(7301748782892921099)
XLA Ops:
  0.6 2.6 %shard_map.136 = (bf16[128,2,1664]{2,1,0:T(2,128)(2,1)}, bf16[256,64]{1,0:T(8,128)(2,1)}, s32[16,2]{1,0:T(8,128)}, s32[2,16]{1,0:T(2,128)}) custom-call(s32[16,2,128]{2,1,0:T(2,128)} %bitcast.26, f32[64,1536]{1,0:T(8,128)} %depth.1, f32[8,13]{1,0:T(8,128)} %bitcast.22), custom_call_target="tpu_custom_call" | custom-call | tf_op jit(solution)/shard_map/pallas_call | solution.py:295
  3.2 0.0 copy-start
  3.2 0.0 copy-start.1
  3.2 0.0 copy-start.6
  3.2 0.0 copy-start.10
  3.2 28.1 %all_to_all.20 = bf16[128,2,1664]{2,1,0:T(2,128)(2,1)S(1)} all-to-all(bf16[128,2,1664]{2,1,0:T(2,128)(2,1)} %get-tuple-element.23), channel_id=1, replica_groups=mesh['view'=16,'edge'=8] {'edge','view'}, dimensions={0} | all-to-all | bytes 1703936 | tf_op jit(solution)/shard_map/all_to_all | solution.py:309
  31.4 0.0 copy-done.10
  31.4 2.5 %shard_map.137 = bf16[8,16,2,1664]{3,2,1,0:T(2,128)(2,1)S(1)} custom-call(bf16[8,16,2,1664]{3,2,1,0:T(2,128)(2,1)S(1)} %bitcast.20, s32[16,2]{1,0:T(8,128)S(1)} %copy-done.6, s32[2,16]{1,0:T(2,128)S(1)} %copy-done.10, bf16[3,16,12288]{2,1,0:T(8,128)(2,1)S(1)} %bitcast.16, bf16[16,12288]{1,0:T(8,128)(2,1)S(1)} %copy-done.1), custom_call_target="tpu_custom_call" | custom-call | tf_op jit(solution)/shard_map/pallas_call | solution.py:310
  33.9 0.0 copy-start.2
  33.9 0.0 copy-start.3
  33.9 0.0 copy-start.4
  33.9 0.0 copy-start.5
  34.0 0.0 copy-start.7
  34.0 0.0 copy-start.8
  34.0 0.0 copy-start.9
  34.0 21.1 %all_to_all.21.incoming = bf16[128,2,1664]{2,1,0:T(2,128)(2,1)S(1)} all-to-all(bf16[128,2,1664]{2,1,0:T(2,128)(2,1)S(1)} %bitcast.21), channel_id=1, replica_groups=mesh['view'=16,'edge'=8] {'edge','view'}, dimensions={0} | all-to-all | bytes 1703936 | tf_op jit(solution)/shard_map/all_to_all | solution.py:318
  55.1 0.0 copy-done.4
  55.1 0.0 copy-done.5
  55.1 0.0 copy-done.7
  55.2 0.8 shard_map.138
  56.0 21.0 %all_to_all.22 = bf16[128,2,1664]{2,1,0:T(2,128)(2,1)S(1)} all-to-all(bf16[128,2,1664]{2,1,0:T(2,128)(2,1)S(1)} %get-tuple-element.27), channel_id=1, replica_groups=mesh['view'=16,'edge'=8] {'edge','view'}, dimensions={0} | all-to-all | bytes 1703936 | tf_op jit(solution)/shard_map/all_to_all | solution.py:309
  77.0 2.5 %shard_map.139 = bf16[8,16,2,1664]{3,2,1,0:T(2,128)(2,1)S(1)} custom-call(bf16[8,16,2,1664]{3,2,1,0:T(2,128)(2,1)S(1)} %bitcast.18, s32[16,2]{1,0:T(8,128)S(1)} %copy-done.6, s32[2,16]{1,0:T(2,128)S(1)} %copy-done.10, bf16[3,16,12288]{2,1,0:T(8,128)(2,1)S(1)} %bitcast.17, bf16[16,12288]{1,0:T(8,128)(2,1)S(1)} %copy-done.1), custom_call_target="tpu_custom_call" | custom-call | tf_op jit(solution)/shard_map/pallas_call | solution.py:310
  79.5 21.0 %all_to_all.23.incoming = bf16[128,2,1664]{2,1,0:T(2,128)(2,1)S(1)} all-to-all(bf16[128,2,1664]{2,1,0:T(2,128)(2,1)S(1)} %bitcast.19), channel_id=1, replica_groups=mesh['view'=16,'edge'=8] {'edge','view'}, dimensions={0} | all-to-all | bytes 1703936 | tf_op jit(solution)/shard_map/all_to_all | solution.py:318
  100.5 1.6 %shard_map.140 = (f32[64,1536]{1,0:T(8,128)}, f32[64,1536]{1,0:T(8,128)}, f32[64,1536]{1,0:T(8,128)}, f32[8,13]{1,0:T(8,128)}, f32[8,13]{1,0:T(8,128)}, /*index=5*/f32[8,13]{1,0:T(8,128)}) custom-call(bf16[128,2,1664]{2,1,0:T(2,128)(2,1)S(1)} %all_to_all.23.incoming, bf16[256,64]{1,0:T(8,128)(2,1)S(1)} %copy-done.5, f32[64,1536]{1,0:T(8,128)S(1)} %get-tuple-element.28.depth, ...), custom_call_target="tpu_custom_call" | custom-call | tf_op jit(solution)/shard_map/pallas_call | solution.py:322
  (7 shorter events, 0.0 us)
Async XLA Ops:
  3.2 28.2 %copy-start = (bf16[16,3,12288]{2,0,1:T(8,128)(2,1)S(1)}, bf16[16,3,12288]{2,0,1:T(8,128)(2,1)}, u32[]{:S(2)}) copy-start(bf16[16,3,12288]{2,0,1:T(8,128)(2,1)} %param.16) | copy-start | bytes 3538948
  3.2 28.2 %copy-start.1 = (bf16[16,12288]{1,0:T(8,128)(2,1)S(1)}, bf16[16,12288]{1,0:T(8,128)(2,1)}, u32[]{:S(2)}) copy-start(bf16[16,12288]{1,0:T(8,128)(2,1)} %conf.3) | copy-start | bytes 1179652
  3.2 28.2 %copy-start.6 = (s32[16,2]{1,0:T(8,128)S(1)}, s32[16,2]{1,0:T(8,128)}, u32[]{:S(2)}) copy-start(s32[16,2]{1,0:T(8,128)} %get-tuple-element.24.mine) | copy-start | bytes 388
  3.2 28.2 %copy-start.10 = (s32[2,16]{1,0:T(2,128)S(1)}, s32[2,16]{1,0:T(2,128)}, u32[]{:S(2)}) copy-start(s32[2,16]{1,0:T(2,128)} %get-tuple-element.25.mine_t) | copy-start | bytes 388
  33.9 21.2 %copy-start.2 = (f32[64,1536]{1,0:T(8,128)S(1)}, f32[64,1536]{1,0:T(8,128)}, u32[]{:S(2)}) copy-start(f32[64,1536]{1,0:T(8,128)} %depth.1) | copy-start | bytes 1179652
  33.9 21.2 %copy-start.3 = (f32[64,1536]{1,0:T(8,128)S(1)}, f32[64,1536]{1,0:T(8,128)}, u32[]{:S(2)}) copy-start(f32[64,1536]{1,0:T(8,128)} %m.1) | copy-start | bytes 1179652
  33.9 21.2 %copy-start.4 = (f32[64,1536]{1,0:T(8,128)S(1)}, f32[64,1536]{1,0:T(8,128)}, u32[]{:S(2)}) copy-start(f32[64,1536]{1,0:T(8,128)} %v.1) | copy-start | bytes 1179652
  33.9 21.2 %copy-start.5 = (bf16[256,64]{1,0:T(8,128)(2,1)S(1)}, bf16[256,64]{1,0:T(8,128)(2,1)}, u32[]{:S(2)}) copy-start(bf16[256,64]{1,0:T(8,128)(2,1)} %get-tuple-element.26.picker) | copy-start | bytes 98308
  34.0 21.2 %copy-start.7 = (f32[13,8]{0,1:T(8,128)S(1)}, f32[13,8]{0,1:T(8,128)}, u32[]{:S(2)}) copy-start(f32[13,8]{0,1:T(8,128)} %param.12) | copy-start | bytes 1252
  34.0 21.2 %copy-start.8 = (f32[13,8]{0,1:T(8,128)S(1)}, f32[13,8]{0,1:T(8,128)}, u32[]{:S(2)}) copy-start(f32[13,8]{0,1:T(8,128)} %param.13) | copy-start | bytes 1252
  34.0 21.2 %copy-start.9 = (f32[13,8]{0,1:T(8,128)S(1)}, f32[13,8]{0,1:T(8,128)}, u32[]{:S(2)}) copy-start(f32[13,8]{0,1:T(8,128)} %param.14) | copy-start | bytes 1252

commit v4 on v3

--- a/solution.py
+++ b/solution.py
@@ -14,6 +14,9 @@
 ROWS = 13
 LANES = 128
 CAP = 2
+CORES = 2
+SHARDS = 8
+ORDER = ("z", "x", "y", "core")
 
 learn_rate = 0.01
 beta_first = 0.9
@@ -56,8 +59,10 @@
     value = jnp.where((local >= 0) & (local < views), local + 1, 0).astype(f32).astype(bf16)
     row = iota((slots, LANES), 0)
     lane = iota((slots, LANES), 1)
-    spread = dot(hot(row[:, :lines] // CAP % lines == lane[:, :lines]), value)
-    hit = (spread > 0.5) & (lane // 16 == row // (CAP * lines))
+    spread = dot(hot(row[:, :lines] // (CAP * CORES) % lines == lane[:, :lines]), value)
+    place = row // CAP
+    shard = place // (CORES * lines) * CORES + place % CORES
+    hit = (spread > 0.5) & (lane // 16 == shard)
     tri = hot(iota((LANES, LANES), 0) < iota((LANES, LANES), 1))
     rank = dot(hot(hit), tri)
     mine = hit & (rank == (row % CAP).astype(f32))
@@ -104,7 +109,7 @@
         copy.start()
     copies[0].wait()
     views = depth.shape[0]
-    picker = make_picker(pairs[:, 1, :], lax.axis_index("view") * views, views)
+    picker = make_picker(pairs[:, 1, :], lax.axis_index(("x", "y")) * views, views)
     picker_out[...] = picker
     copies[1].wait()
     row = spread_pose(pose_t[...])
@@ -112,7 +117,7 @@
     send_rows(out, picker, depth[...], row)
 
     edges = mine.shape[0]
-    me = lax.axis_index("view") * lax.axis_size("edge") + lax.axis_index("edge")
+    me = lax.axis_index(("x", "y")) * SHARDS + lax.axis_index(("z", "core"))
     line = pairs[me // (LANES // edges)].astype(f32)
     lanes = iota((edges, LANES), 1)
     pick = (lanes == me % (LANES // edges) * edges + iota((edges, LANES), 0)).astype(f32)
@@ -141,16 +146,18 @@
 
 
 def edge_kernel(arrived, mine, mine_t, points, conf, out, depth_s, grad_s):
-    shards, groups, cap, width = arrived.shape
+    planes, groups, cores, cap, width = arrived.shape
+    shards = planes * cores
     pixels = width - LANES
     edges = mine.shape[0]
     slots = shards * groups * cap
 
     def place(view):
-        return view // 8 % shards * groups + view // (8 * shards)
+        shard = view // 8 % shards
+        return (shard // cores * groups + view // (8 * shards)) * cores + shard % cores
 
     both = jnp.concatenate([mine[:, 0:1], mine[:, 1:2]], axis=0)
-    pose_rows = arrived[:, :, :, pixels:].reshape(slots, LANES)
+    pose_rows = arrived[:, :, :, :, pixels:].reshape(slots, LANES)
     slot_of = iota((2 * edges, slots), 1)
     lane_mask = iota((2 * edges, LANES), 1) % 8 == both % 8
     fold = hot(iota((LANES, LANES), 0) // 8 == iota((LANES, LANES), 1))
@@ -166,7 +173,7 @@
     slot = jnp.sum(jnp.where((group == group_row) & earlier, 1.0, 0.0), axis=1, keepdims=True)
     sel = hot((group * cap).astype(f32) + slot == iota((edges, groups * cap), 1).astype(f32))
     for s in range(shards):
-        rows = arrived[s, :, :, :pixels].reshape(groups * cap, pixels)
+        rows = arrived[s // cores, :, s % cores, :, :pixels].reshape(groups * cap, pixels)
         depth_s[:, s * pixels : (s + 1) * pixels] = jnp.exp(dot(sel, rows))
 
     pf = [poses[:edges, k : k + 1] for k in range(12)]
@@ -195,9 +202,9 @@
 
     def step(i, sums):
         s_acc, d_acc, e_acc = list(sums[:3]), list(sums[3:12]), list(sums[12:])
-        rise = [slope[a] * i.astype(f32) for a in range(3)]
+        rise = [slope[a] * float(i) for a in range(3)]
         for k in range(3):
-            at = pl.ds(pl.multiple_of(i * period + k * LANES, LANES), LANES)
+            at = pl.ds(i * period + k * LANES, LANES)
             dep = depth_s[:, at]
             weight = conf[:, at].astype(f32)
             grad = None
@@ -214,7 +221,12 @@
         return (*s_acc, *d_acc, *e_acc)
 
     steps = shards * pixels // period
-    sums = lax.fori_loop(0, steps, step, (jnp.zeros(tile, f32),) * 15, unroll=4)
+    sums = (jnp.zeros(tile, f32),) * 15
+    for s in range(shards):
+        for i in range(steps // shards):
+            sums = step(s * (steps // shards) + i, sums)
+        placed = dot(sel, grad_s[:, s * pixels : (s + 1) * pixels], ((0,), (0,))).astype(bf16)
+        out[s // cores, :, s % cores, :, :pixels] = placed.reshape(groups, cap, pixels)
 
     def total(x):
         return jnp.sum(x, axis=1, keepdims=True)
@@ -231,10 +243,6 @@
         )
         for a in range(3)
     ]
-
-    for s in range(shards):
-        placed = dot(sel, grad_s[:, s * pixels : (s + 1) * pixels], ((0,), (0,))).astype(bf16)
-        out[s, :, :, :pixels] = placed.reshape(groups, cap, pixels)
 
     moments = [[u_sum[a] * inv_f, v_sum[a] * inv_f, d_sum[a]] for a in range(3)]
     grad_first = [None] * 12
@@ -260,7 +268,7 @@
     both_row = jnp.concatenate([mine_t[0:1, :], mine_t[1:2, :]], axis=1)
     owner_hot = hot(iota((slots, 2 * edges), 0) // cap == place(both_row))
     owned = dot(owner_hot, lead) + dot(owner_hot, rest)
-    out[:, :, :, pixels:] = two_parts(owned).reshape(shards, groups, cap, LANES)
+    out[:, :, :, :, pixels:] = two_parts(owned).reshape(planes, groups, cores, cap, LANES)
 
 
 def call(kernel, outs, scratch=(), in_specs=None, mib=40):
@@ -275,8 +283,8 @@
 
 
 def shards(log_depth, depth_m, depth_v, pose, pose_m, pose_v, pairs, points, conf):
-    n_view = lax.axis_size("view")
-    n_edge = lax.axis_size("edge")
+    n_view = lax.axis_size("x") * lax.axis_size("y")
+    n_edge = lax.axis_size("z") * lax.axis_size("core")
     owners = n_view * n_edge
     views, pixels = log_depth.shape
     edges = points.shape[0]
@@ -286,7 +294,7 @@
     message = S((owners, CAP, width), bf16)
     depth_out = [S((views, pixels), f32)] * 3
     exchange = functools.partial(
-        lax.all_to_all, axis_name=("edge", "view"), split_axis=0, concat_axis=0, tiled=True
+        lax.all_to_all, axis_name=ORDER, split_axis=0, concat_axis=0, tiled=True
     )
 
     poses = [pose.T, pose_m.T, pose_v.T]
@@ -306,10 +314,10 @@
     )(pairs.T.reshape(2, -1, LANES).transpose(1, 0, 2), log_depth, poses[0])
     planes = points.transpose(1, 0, 2)
     for turn in range(ITERS):
-        arrived = exchange(sending).reshape(n_edge, n_view, CAP, width)
+        arrived = exchange(sending).reshape(n_edge // CORES, n_view, CORES, CAP, width)
         back = call(
             edge_kernel,
-            S((n_edge, n_view, CAP, width), bf16),
+            S((n_edge // CORES, n_view, CORES, CAP, width), bf16),
             [
                 pltpu.VMEM((edges, pixels * n_edge), f32),
                 pltpu.VMEM((edges, pixels * n_edge), bf16),
@@ -329,8 +337,10 @@
 
 
 def solution(mesh):
-    depth = P("view", "edge")
-    pose = P(None, ("view", "edge"))
-    in_specs = (depth,) * 3 + (pose,) * 3 + (P(), P(("view", "edge"), None, None), P(("view", "edge"), None))
+    grid = jax.sharding.Mesh(mesh.devices.reshape(4, 4, SHARDS // CORES, CORES), ("x", "y", "z", "core"))
+    view, edge = ("x", "y"), ("z", "core")
+    depth = P(view, edge)
+    pose = P(None, view + edge)
+    in_specs = (depth,) * 3 + (pose,) * 3 + (P(), P(view + edge, None, None), P(view + edge, None))
     out_specs = (depth,) * 3 + (pose,) * 3
-    return jax.shard_map(shards, mesh=mesh, in_specs=in_specs, out_specs=out_specs, check_vma=False)
+    return jax.shard_map(shards, mesh=grid, in_specs=in_specs, out_specs=out_specs, check_vma=False)

time: 102 us -> 103 us (level)
  no operation moved by 1% of the time
where the time goes in v4:
time: 103 us
  blocking collectives  92.2 us (90%)
  Pallas kernels  9.61 us (9%)
    all_to_all x2, blocking collectives, shards(): exchange(sending).reshape(n_edge // CORES, n_view, CORES, CAP, width)  49.6 us
    all_to_all x2, blocking collectives, shards(): incoming = exchange(back.reshape(owners, CAP, width))  42.6 us
    pallas_call x2, Pallas kernels, shards(): call(edge_kernel, S((n_edge // CORES, n_view, CORES, CAP, width), bf16),...  4.67 us
    pallas_call x1, Pallas kernels, shards(): call(first_kernel, [message, S((owners * CAP, views), bf16), S((edges, 2)...  2.56 us
    pallas_call x2, Pallas kernels, shards(): call(kernel, depth_out + pose_out + ([] if last else [message]))  2.38 us

profile of v4, /device:TPU:1, one launch (start us, length us, event | category | flops | bytes accessed | tf_op | source)
XLA Modules:
  0.0 102.7 jit_solution(14740347518226644812)
XLA Ops:
  0.6 2.6 %shard_map.136 = (bf16[128,2,1664]{2,1,0:T(2,128)(2,1)}, bf16[256,64]{1,0:T(8,128)(2,1)}, s32[16,2]{1,0:T(8,128)}, s32[2,16]{1,0:T(2,128)}) custom-call(s32[16,2,128]{2,1,0:T(2,128)} %bitcast.26, f32[64,1536]{1,0:T(8,128)} %depth.1, f32[8,13]{1,0:T(8,128)} %bitcast.22), custom_call_target="tpu_custom_call" | custom-call | tf_op jit(solution)/shard_map/pallas_call | solution.py:303
  3.2 0.0 copy-start
  3.2 0.0 copy-start.1
  3.2 0.0 copy-start.6
  3.2 0.0 copy-start.10
  3.2 28.3 %all_to_all.20 = bf16[128,2,1664]{2,1,0:T(2,128)(2,1)S(1)} all-to-all(bf16[128,2,1664]{2,1,0:T(2,128)(2,1)} %get-tuple-element.23), channel_id=1, replica_groups=mesh['x'=4,'y'=4,'z'=4,'core'=2] {'z','x','y','core'}, dimensions={0} | all-to-all | bytes 1703936 | tf_op jit(solution)/shard_map/all_to_all | solution.py:317
  31.6 0.0 copy-done
  31.6 0.0 copy-done.1
  31.6 0.0 copy-done.6
  31.6 2.3 %shard_map.137 = bf16[4,16,2,2,1664]{4,3,2,1,0:T(2,128)(2,1)S(1)} custom-call(bf16[4,16,2,2,1664]{4,3,2,1,0:T(2,128)(2,1)S(1)} %bitcast.20, s32[16,2]{1,0:T(8,128)S(1)} %copy-done.6, s32[2,16]{1,0:T(2,128)S(1)} %copy-done.10, bf16[3,16,12288]{2,1,0:T(8,128)(2,1)S(1)} %bitcast.16, bf16[16,12288]{1,0:T(8,128)(2,1)S(1)} %copy-done.1), custom_call_target="tpu_custom_call" | custom-call | tf_op jit(solution)/shard_map/pallas_call | solution.py:318
  33.9 0.0 copy-start.2
  34.0 0.0 copy-start.3
  34.0 0.0 copy-start.4
  34.0 0.0 copy-start.5
  34.0 0.0 copy-start.7
  34.0 0.0 copy-start.8
  34.0 0.0 copy-start.9
  34.0 21.3 %all_to_all.21.incoming = bf16[128,2,1664]{2,1,0:T(2,128)(2,1)S(1)} all-to-all(bf16[128,2,1664]{2,1,0:T(2,128)(2,1)S(1)} %bitcast.21), channel_id=1, replica_groups=mesh['x'=4,'y'=4,'z'=4,'core'=2] {'z','x','y','core'}, dimensions={0} | all-to-all | bytes 1703936 | tf_op jit(solution)/shard_map/all_to_all | solution.py:326
  55.3 0.0 copy-done.2
  55.4 0.8 shard_map.138
  56.2 21.3 %all_to_all.22 = bf16[128,2,1664]{2,1,0:T(2,128)(2,1)S(1)} all-to-all(bf16[128,2,1664]{2,1,0:T(2,128)(2,1)S(1)} %get-tuple-element.27), channel_id=1, replica_groups=mesh['x'=4,'y'=4,'z'=4,'core'=2] {'z','x','y','core'}, dimensions={0} | all-to-all | bytes 1703936 | tf_op jit(solution)/shard_map/all_to_all | solution.py:317
  77.5 2.3 %shard_map.139 = bf16[4,16,2,2,1664]{4,3,2,1,0:T(2,128)(2,1)S(1)} custom-call(bf16[4,16,2,2,1664]{4,3,2,1,0:T(2,128)(2,1)S(1)} %bitcast.18, s32[16,2]{1,0:T(8,128)S(1)} %copy-done.6, s32[2,16]{1,0:T(2,128)S(1)} %copy-done.10, bf16[3,16,12288]{2,1,0:T(8,128)(2,1)S(1)} %bitcast.17, bf16[16,12288]{1,0:T(8,128)(2,1)S(1)} %copy-done.1), custom_call_target="tpu_custom_call" | custom-call | tf_op jit(solution)/shard_map/pallas_call | solution.py:318
  79.8 21.3 %all_to_all.23.incoming = bf16[128,2,1664]{2,1,0:T(2,128)(2,1)S(1)} all-to-all(bf16[128,2,1664]{2,1,0:T(2,128)(2,1)S(1)} %bitcast.19), channel_id=1, replica_groups=mesh['x'=4,'y'=4,'z'=4,'core'=2] {'z','x','y','core'}, dimensions={0} | all-to-all | bytes 1703936 | tf_op jit(solution)/shard_map/all_to_all | solution.py:326
  101.1 1.6 %shard_map.140 = (f32[64,1536]{1,0:T(8,128)}, f32[64,1536]{1,0:T(8,128)}, f32[64,1536]{1,0:T(8,128)}, f32[8,13]{1,0:T(8,128)}, f32[8,13]{1,0:T(8,128)}, /*index=5*/f32[8,13]{1,0:T(8,128)}) custom-call(bf16[128,2,1664]{2,1,0:T(2,128)(2,1)S(1)} %all_to_all.23.incoming, bf16[256,64]{1,0:T(8,128)(2,1)S(1)} %copy-done.5, f32[64,1536]{1,0:T(8,128)S(1)} %get-tuple-element.28.depth, ...), custom_call_target="tpu_custom_call" | custom-call | tf_op jit(solution)/shard_map/pallas_call | solution.py:330
  (7 shorter events, 0.0 us)
Async XLA Ops:
  3.2 28.4 %copy-start = (bf16[16,3,12288]{2,0,1:T(8,128)(2,1)S(1)}, bf16[16,3,12288]{2,0,1:T(8,128)(2,1)}, u32[]{:S(2)}) copy-start(bf16[16,3,12288]{2,0,1:T(8,128)(2,1)} %param.16) | copy-start | bytes 3538948
  3.2 28.4 %copy-start.1 = (bf16[16,12288]{1,0:T(8,128)(2,1)S(1)}, bf16[16,12288]{1,0:T(8,128)(2,1)}, u32[]{:S(2)}) copy-start(bf16[16,12288]{1,0:T(8,128)(2,1)} %conf.3) | copy-start | bytes 1179652
  3.2 28.4 %copy-start.6 = (s32[16,2]{1,0:T(8,128)S(1)}, s32[16,2]{1,0:T(8,128)}, u32[]{:S(2)}) copy-start(s32[16,2]{1,0:T(8,128)} %get-tuple-element.24.mine) | copy-start | bytes 388
  3.2 28.4 %copy-start.10 = (s32[2,16]{1,0:T(2,128)S(1)}, s32[2,16]{1,0:T(2,128)}, u32[]{:S(2)}) copy-start(s32[2,16]{1,0:T(2,128)} %get-tuple-element.25.mine_t) | copy-start | bytes 388
  33.9 21.4 %copy-start.2 = (f32[64,1536]{1,0:T(8,128)S(1)}, f32[64,1536]{1,0:T(8,128)}, u32[]{:S(2)}) copy-start(f32[64,1536]{1,0:T(8,128)} %depth.1) | copy-start | bytes 1179652
  34.0 21.4 %copy-start.3 = (f32[64,1536]{1,0:T(8,128)S(1)}, f32[64,1536]{1,0:T(8,128)}, u32[]{:S(2)}) copy-start(f32[64,1536]{1,0:T(8,128)} %m.1) | copy-start | bytes 1179652
  34.0 21.3 %copy-start.4 = (f32[64,1536]{1,0:T(8,128)S(1)}, f32[64,1536]{1,0:T(8,128)}, u32[]{:S(2)}) copy-start(f32[64,1536]{1,0:T(8,128)} %v.1) | copy-start | bytes 1179652
  34.0 21.3 %copy-start.5 = (bf16[256,64]{1,0:T(8,128)(2,1)S(1)}, bf16[256,64]{1,0:T(8,128)(2,1)}, u32[]{:S(2)}) copy-start(bf16[256,64]{1,0:T(8,128)(2,1)} %get-tuple-element.26.picker) | copy-start | bytes 98308
  34.0 21.3 %copy-start.7 = (f32[13,8]{0,1:T(8,128)S(1)}, f32[13,8]{0,1:T(8,128)}, u32[]{:S(2)}) copy-start(f32[13,8]{0,1:T(8,128)} %param.12) | copy-start | bytes 1252
  34.0 21.3 %copy-start.8 = (f32[13,8]{0,1:T(8,128)S(1)}, f32[13,8]{0,1:T(8,128)}, u32[]{:S(2)}) copy-start(f32[13,8]{0,1:T(8,128)} %param.13) | copy-start | bytes 1252
  34.0 21.3 %copy-start.9 = (f32[13,8]{0,1:T(8,128)S(1)}, f32[13,8]{0,1:T(8,128)}, u32[]{:S(2)}) copy-start(f32[13,8]{0,1:T(8,128)} %param.14) | copy-start | bytes 1252

commit v5 on v3

--- a/solution.py
+++ b/solution.py
@@ -195,9 +195,9 @@
 
     def step(i, sums):
         s_acc, d_acc, e_acc = list(sums[:3]), list(sums[3:12]), list(sums[12:])
-        rise = [slope[a] * i.astype(f32) for a in range(3)]
+        rise = [slope[a] * float(i) for a in range(3)]
         for k in range(3):
-            at = pl.ds(pl.multiple_of(i * period + k * LANES, LANES), LANES)
+            at = pl.ds(i * period + k * LANES, LANES)
             dep = depth_s[:, at]
             weight = conf[:, at].astype(f32)
             grad = None
@@ -214,7 +214,12 @@
         return (*s_acc, *d_acc, *e_acc)
 
     steps = shards * pixels // period
-    sums = lax.fori_loop(0, steps, step, (jnp.zeros(tile, f32),) * 15, unroll=4)
+    sums = (jnp.zeros(tile, f32),) * 15
+    for s in range(shards):
+        for i in range(steps // shards):
+            sums = step(s * (steps // shards) + i, sums)
+        placed = dot(sel, grad_s[:, s * pixels : (s + 1) * pixels], ((0,), (0,))).astype(bf16)
+        out[s, :, :, :pixels] = placed.reshape(groups, cap, pixels)
 
     def total(x):
         return jnp.sum(x, axis=1, keepdims=True)
@@ -231,10 +236,6 @@
         )
         for a in range(3)
     ]
-
-    for s in range(shards):
-        placed = dot(sel, grad_s[:, s * pixels : (s + 1) * pixels], ((0,), (0,))).astype(bf16)
-        out[s, :, :, :pixels] = placed.reshape(groups, cap, pixels)
 
     moments = [[u_sum[a] * inv_f, v_sum[a] * inv_f, d_sum[a]] for a in range(3)]
     grad_first = [None] * 12
@@ -302,8 +303,8 @@
             pltpu.SemaphoreType.DMA((3,)),
         ],
         [hbm, hbm, hbm],
-        64,
-    )(pairs.T.reshape(2, -1, LANES).transpose(1, 0, 2), log_depth, poses[0])
+        40,
+    )(*[pltpu.with_memory_space_constraint(x, pltpu.HBM) for x in (pairs.T.reshape(2, -1, LANES).transpose(1, 0, 2), log_depth, poses[0])])
     planes = points.transpose(1, 0, 2)
     for turn in range(ITERS):
         arrived = exchange(sending).reshape(n_edge, n_view, CAP, width)

time: 102 us -> 101 us (level)
  Pallas kernels: 9.94 us -> 8.85 us
where the time goes in v5:
time: 101 us
  blocking collectives  91 us (90%)
  Pallas kernels  8.85 us (9%)
    all_to_all x2, blocking collectives, shards(): arrived = exchange(sending).reshape(n_edge, n_view, CAP, width)  48.9 us
    all_to_all x2, blocking collectives, shards(): incoming = exchange(back.reshape(owners, CAP, width))  42.1 us
    pallas_call x2, Pallas kernels, shards(): call(edge_kernel, S((n_edge, n_view, CAP, width), bf16), [pltpu.VMEM((edg...  4.66 us
    pallas_call x2, Pallas kernels, shards(): call(kernel, depth_out + pose_out + ([] if last else [message]))  2.39 us

profile of v5, /device:TPU:1, one launch (start us, length us, event | category | flops | bytes accessed | tf_op | source)
XLA Modules:
  0.0 100.7 jit_solution(15688603975558863133)
XLA Ops:
  0.6 0.0 copy-start.1
  0.6 0.0 copy-start
  0.7 1.8 %shard_map.136 = (bf16[128,2,1664]{2,1,0:T(2,128)(2,1)S(1)}, bf16[256,64]{1,0:T(8,128)(2,1)S(1)}, s32[16,2]{1,0:T(8,128)S(1)}, s32[2,16]{1,0:T(2,128)S(1)}) custom-call(s32[16,2,128]{2,1,0:T(2,128)} %bitcast.26, f32[64,1536]{1,0:T(8,128)} %depth.1, f32[8,13]{1,0:T(8,128)} %bitcast.22), custom_call_target="tpu_custom_call" | custom-call | tf_op jit(solution)/shard_map/pallas_call | solution.py:296
  2.5 27.9 %all_to_all.20 = bf16[128,2,1664]{2,1,0:T(2,128)(2,1)S(1)} all-to-all(bf16[128,2,1664]{2,1,0:T(2,128)(2,1)S(1)} %get-tuple-element.23), channel_id=1, replica_groups=mesh['view'=16,'edge'=8] {'edge','view'}, dimensions={0} | all-to-all | bytes 1703936 | tf_op jit(solution)/shard_map/all_to_all | solution.py:310
  30.4 0.0 copy-done.1
  30.4 0.0 copy-done
  30.4 2.3 %shard_map.137 = bf16[8,16,2,1664]{3,2,1,0:T(2,128)(2,1)S(1)} custom-call(bf16[8,16,2,1664]{3,2,1,0:T(2,128)(2,1)S(1)} %bitcast.20, s32[16,2]{1,0:T(8,128)S(1)} %get-tuple-element.24.mine, s32[2,16]{1,0:T(2,128)S(1)} %get-tuple-element.25.mine_t, bf16[3,16,12288]{2,1,0:T(8,128)(2,1)S(1)} %bitcast.16, bf16[16,12288]{1,0:T(8,128)(2,1)S(1)} %copy-done.1), custom_call_target="tpu_custom_call" | custom-call | tf_op jit(solution)/shard_map/pallas_call | solution.py:311
  32.7 0.0 copy-start.2
  32.8 0.0 copy-start.3
  32.8 0.0 copy-start.4
  32.8 0.0 copy-start.5
  32.8 0.0 copy-start.6
  32.8 0.0 copy-start.7
  32.8 21.1 %all_to_all.21.incoming = bf16[128,2,1664]{2,1,0:T(2,128)(2,1)S(1)} all-to-all(bf16[128,2,1664]{2,1,0:T(2,128)(2,1)S(1)} %bitcast.21), channel_id=1, replica_groups=mesh['view'=16,'edge'=8] {'edge','view'}, dimensions={0} | all-to-all | bytes 1703936 | tf_op jit(solution)/shard_map/all_to_all | solution.py:319
  53.9 0.0 copy-done.2
  53.9 0.0 copy-done.3
  53.9 0.0 copy-done.4
  53.9 0.0 copy-done.5
  54.0 0.0 copy-done.6
  54.0 0.8 shard_map.138
  54.8 21.0 %all_to_all.22 = bf16[128,2,1664]{2,1,0:T(2,128)(2,1)S(1)} all-to-all(bf16[128,2,1664]{2,1,0:T(2,128)(2,1)S(1)} %get-tuple-element.27), channel_id=1, replica_groups=mesh['view'=16,'edge'=8] {'edge','view'}, dimensions={0} | all-to-all | bytes 1703936 | tf_op jit(solution)/shard_map/all_to_all | solution.py:310
  75.8 2.3 %shard_map.139 = bf16[8,16,2,1664]{3,2,1,0:T(2,128)(2,1)S(1)} custom-call(bf16[8,16,2,1664]{3,2,1,0:T(2,128)(2,1)S(1)} %bitcast.18, s32[16,2]{1,0:T(8,128)S(1)} %get-tuple-element.24.mine, s32[2,16]{1,0:T(2,128)S(1)} %get-tuple-element.25.mine_t, bf16[3,16,12288]{2,1,0:T(8,128)(2,1)S(1)} %bitcast.17, bf16[16,12288]{1,0:T(8,128)(2,1)S(1)} %copy-done.1), custom_call_target="tpu_custom_call" | custom-call | tf_op jit(solution)/shard_map/pallas_call | solution.py:311
  78.1 21.0 %all_to_all.23.incoming = bf16[128,2,1664]{2,1,0:T(2,128)(2,1)S(1)} all-to-all(bf16[128,2,1664]{2,1,0:T(2,128)(2,1)S(1)} %bitcast.19), channel_id=1, replica_groups=mesh['view'=16,'edge'=8] {'edge','view'}, dimensions={0} | all-to-all | bytes 1703936 | tf_op jit(solution)/shard_map/all_to_all | solution.py:319
  99.1 1.6 %shard_map.140 = (f32[64,1536]{1,0:T(8,128)}, f32[64,1536]{1,0:T(8,128)}, f32[64,1536]{1,0:T(8,128)}, f32[8,13]{1,0:T(8,128)}, f32[8,13]{1,0:T(8,128)}, /*index=5*/f32[8,13]{1,0:T(8,128)}) custom-call(bf16[128,2,1664]{2,1,0:T(2,128)(2,1)S(1)} %all_to_all.23.incoming, bf16[256,64]{1,0:T(8,128)(2,1)S(1)} %get-tuple-element.26.picker, ...), custom_call_target="tpu_custom_call" | custom-call | tf_op jit(solution)/shard_map/pallas_call | solution.py:323
  (1 shorter events, 0.0 us)
Async XLA Ops:
  0.6 29.8 %copy-start.1 = (bf16[16,12288]{1,0:T(8,128)(2,1)S(1)}, bf16[16,12288]{1,0:T(8,128)(2,1)}, u32[]{:S(2)}) copy-start(bf16[16,12288]{1,0:T(8,128)(2,1)} %conf.3) | copy-start | bytes 1179652
  0.6 29.8 %copy-start = (bf16[16,3,12288]{2,0,1:T(8,128)(2,1)S(1)}, bf16[16,3,12288]{2,0,1:T(8,128)(2,1)}, u32[]{:S(2)}) copy-start(bf16[16,3,12288]{2,0,1:T(8,128)(2,1)} %param.16) | copy-start | bytes 3538948
  32.7 21.2 %copy-start.2 = (f32[64,1536]{1,0:T(8,128)S(1)}, f32[64,1536]{1,0:T(8,128)}, u32[]{:S(2)}) copy-start(f32[64,1536]{1,0:T(8,128)} %depth.1) | copy-start | bytes 1179652
  32.8 21.2 %copy-start.3 = (f32[64,1536]{1,0:T(8,128)S(1)}, f32[64,1536]{1,0:T(8,128)}, u32[]{:S(2)}) copy-start(f32[64,1536]{1,0:T(8,128)} %m.1) | copy-start | bytes 1179652
  32.8 21.2 %copy-start.4 = (f32[64,1536]{1,0:T(8,128)S(1)}, f32[64,1536]{1,0:T(8,128)}, u32[]{:S(2)}) copy-start(f32[64,1536]{1,0:T(8,128)} %v.1) | copy-start | bytes 1179652
  32.8 21.2 %copy-start.5 = (f32[13,8]{0,1:T(8,128)S(1)}, f32[13,8]{0,1:T(8,128)}, u32[]{:S(2)}) copy-start(f32[13,8]{0,1:T(8,128)} %param.12) | copy-start | bytes 1252
  32.8 21.2 %copy-start.6 = (f32[13,8]{0,1:T(8,128)S(1)}, f32[13,8]{0,1:T(8,128)}, u32[]{:S(2)}) copy-start(f32[13,8]{0,1:T(8,128)} %param.13) | copy-start | bytes 1252
  32.8 21.2 %copy-start.7 = (f32[13,8]{0,1:T(8,128)S(1)}, f32[13,8]{0,1:T(8,128)}, u32[]{:S(2)}) copy-start(f32[13,8]{0,1:T(8,128)} %param.14) | copy-start | bytes 1252

commit v6 on v4

--- a/solution.py
+++ b/solution.py
@@ -14,9 +14,9 @@
 ROWS = 13
 LANES = 128
 CAP = 2
-CORES = 2
 SHARDS = 8
-ORDER = ("z", "x", "y", "core")
+SIDE = 4
+ORDER = ("y", "z", "core", "x")
 
 learn_rate = 0.01
 beta_first = 0.9
@@ -59,10 +59,10 @@
     value = jnp.where((local >= 0) & (local < views), local + 1, 0).astype(f32).astype(bf16)
     row = iota((slots, LANES), 0)
     lane = iota((slots, LANES), 1)
-    spread = dot(hot(row[:, :lines] // (CAP * CORES) % lines == lane[:, :lines]), value)
     place = row // CAP
-    shard = place // (CORES * lines) * CORES + place % CORES
-    hit = (spread > 0.5) & (lane // 16 == shard)
+    block = place % SIDE * SIDE + place // (SIDE * SHARDS)
+    spread = dot(hot(block[:, :lines] == lane[:, :lines]), value)
+    hit = (spread > 0.5) & (lane // 16 == place // SIDE % SHARDS)
     tri = hot(iota((LANES, LANES), 0) < iota((LANES, LANES), 1))
     rank = dot(hot(hit), tri)
     mine = hit & (rank == (row % CAP).astype(f32))
@@ -146,15 +146,15 @@
 
 
 def edge_kernel(arrived, mine, mine_t, points, conf, out, depth_s, grad_s):
-    planes, groups, cores, cap, width = arrived.shape
-    shards = planes * cores
+    side_y, shards, side_x, cap, width = arrived.shape
+    groups = side_y * side_x
     pixels = width - LANES
     edges = mine.shape[0]
     slots = shards * groups * cap
 
     def place(view):
-        shard = view // 8 % shards
-        return (shard // cores * groups + view // (8 * shards)) * cores + shard % cores
+        block = view // (8 * shards)
+        return (block % side_y * shards + view // 8 % shards) * side_x + block // side_y
 
     both = jnp.concatenate([mine[:, 0:1], mine[:, 1:2]], axis=0)
     pose_rows = arrived[:, :, :, :, pixels:].reshape(slots, LANES)
@@ -168,12 +168,13 @@
         poses = part_poses if poses is None else poses + part_poses
 
     group = mine[:, 1:2] // 64
+    line = group % side_y * side_x + group // side_y
     group_row = mine_t[1:2, :] // 64
     earlier = iota((edges, edges), 1) < iota((edges, edges), 0)
     slot = jnp.sum(jnp.where((group == group_row) & earlier, 1.0, 0.0), axis=1, keepdims=True)
-    sel = hot((group * cap).astype(f32) + slot == iota((edges, groups * cap), 1).astype(f32))
+    sel = hot((line * cap).astype(f32) + slot == iota((edges, groups * cap), 1).astype(f32))
     for s in range(shards):
-        rows = arrived[s // cores, :, s % cores, :, :pixels].reshape(groups * cap, pixels)
+        rows = arrived[:, s, :, :, :pixels].reshape(groups * cap, pixels)
         depth_s[:, s * pixels : (s + 1) * pixels] = jnp.exp(dot(sel, rows))
 
     pf = [poses[:edges, k : k + 1] for k in range(12)]
@@ -226,7 +227,7 @@
         for i in range(steps // shards):
             sums = step(s * (steps // shards) + i, sums)
         placed = dot(sel, grad_s[:, s * pixels : (s + 1) * pixels], ((0,), (0,))).astype(bf16)
-        out[s // cores, :, s % cores, :, :pixels] = placed.reshape(groups, cap, pixels)
+        out[:, s, :, :, :pixels] = placed.reshape(side_y, side_x, cap, pixels)
 
     def total(x):
         return jnp.sum(x, axis=1, keepdims=True)
@@ -268,7 +269,7 @@
     both_row = jnp.concatenate([mine_t[0:1, :], mine_t[1:2, :]], axis=1)
     owner_hot = hot(iota((slots, 2 * edges), 0) // cap == place(both_row))
     owned = dot(owner_hot, lead) + dot(owner_hot, rest)
-    out[:, :, :, :, pixels:] = two_parts(owned).reshape(planes, groups, cores, cap, LANES)
+    out[:, :, :, :, pixels:] = two_parts(owned).reshape(side_y, shards, side_x, cap, LANES)
 
 
 def call(kernel, outs, scratch=(), in_specs=None, mib=40):
@@ -310,14 +311,14 @@
             pltpu.SemaphoreType.DMA((3,)),
         ],
         [hbm, hbm, hbm],
-        64,
-    )(pairs.T.reshape(2, -1, LANES).transpose(1, 0, 2), log_depth, poses[0])
+        40,
+    )(*[pltpu.with_memory_space_constraint(x, pltpu.HBM) for x in (pairs.T.reshape(2, -1, LANES).transpose(1, 0, 2), log_depth, poses[0])])
     planes = points.transpose(1, 0, 2)
     for turn in range(ITERS):
-        arrived = exchange(sending).reshape(n_edge // CORES, n_view, CORES, CAP, width)
+        arrived = exchange(sending).reshape(SIDE, n_edge, SIDE, CAP, width)
         back = call(
             edge_kernel,
-            S((n_edge // CORES, n_view, CORES, CAP, width), bf16),
+            S((SIDE, n_edge, SIDE, CAP, width), bf16),
             [
                 pltpu.VMEM((edges, pixels * n_edge), f32),
                 pltpu.VMEM((edges, pixels * n_edge), bf16),
@@ -337,7 +338,7 @@
 
 
 def solution(mesh):
-    grid = jax.sharding.Mesh(mesh.devices.reshape(4, 4, SHARDS // CORES, CORES), ("x", "y", "z", "core"))
+    grid = jax.sharding.Mesh(mesh.devices.reshape(SIDE, SIDE, SIDE, -1), ("x", "y", "z", "core"))
     view, edge = ("x", "y"), ("z", "core")
     depth = P(view, edge)
     pose = P(None, view + edge)

time: 103 us -> 101 us (0.981)
  no operation moved by 1% of the time
where the time goes in v6:
time: 101 us
  blocking collectives  91.5 us (91%)
  Pallas kernels  8.86 us (9%)
    all_to_all x2, blocking collectives, shards(): arrived = exchange(sending).reshape(SIDE, n_edge, SIDE, CAP, width)  49.8 us
    all_to_all x2, blocking collectives, shards(): incoming = exchange(back.reshape(owners, CAP, width))  41.7 us
    pallas_call x2, Pallas kernels, shards(): call(edge_kernel, S((SIDE, n_edge, SIDE, CAP, width), bf16), [pltpu.VMEM(...  4.68 us
    pallas_call x2, Pallas kernels, shards(): call(kernel, depth_out + pose_out + ([] if last else [message]))  2.38 us

profile of v6, /device:TPU:1, one launch (start us, length us, event | category | flops | bytes accessed | tf_op | source)
XLA Modules:
  0.0 101.2 jit_solution(10033260185466382756)
XLA Ops:
  0.6 0.0 copy-start.1
  0.6 0.0 copy-start
  0.7 1.8 %shard_map.136 = (bf16[128,2,1664]{2,1,0:T(2,128)(2,1)S(1)}, bf16[256,64]{1,0:T(8,128)(2,1)S(1)}, s32[16,2]{1,0:T(8,128)S(1)}, s32[2,16]{1,0:T(2,128)S(1)}) custom-call(s32[16,2,128]{2,1,0:T(2,128)} %bitcast.26, f32[64,1536]{1,0:T(8,128)} %depth.1, f32[8,13]{1,0:T(8,128)} %bitcast.22), custom_call_target="tpu_custom_call" | custom-call | tf_op jit(solution)/shard_map/pallas_call | solution.py:304
  2.5 29.0 %all_to_all.20 = bf16[128,2,1664]{2,1,0:T(2,128)(2,1)S(1)} all-to-all(bf16[128,2,1664]{2,1,0:T(2,128)(2,1)S(1)} %get-tuple-element.23), channel_id=1, replica_groups=mesh['x'=4,'y'=4,'z'=4,'core'=2] {'y','z','core','x'}, dimensions={0} | all-to-all | bytes 1703936 | tf_op jit(solution)/shard_map/all_to_all | solution.py:318
  31.4 0.0 copy-done.1
  31.4 0.0 copy-done
  31.4 2.3 %shard_map.137 = bf16[4,8,4,2,1664]{4,3,2,1,0:T(2,128)(2,1)S(1)} custom-call(bf16[4,8,4,2,1664]{4,3,2,1,0:T(2,128)(2,1)S(1)} %bitcast.20, s32[16,2]{1,0:T(8,128)S(1)} %get-tuple-element.24.mine, s32[2,16]{1,0:T(2,128)S(1)} %get-tuple-element.25.mine_t, bf16[3,16,12288]{2,1,0:T(8,128)(2,1)S(1)} %bitcast.16, bf16[16,12288]{1,0:T(8,128)(2,1)S(1)} %copy-done.1), custom_call_target="tpu_custom_call" | custom-call | tf_op jit(solution)/shard_map/pallas_call | solution.py:319
  33.8 0.0 copy-start.2
  33.8 0.0 copy-start.3
  33.8 0.0 copy-start.4
  33.8 0.0 copy-start.5
  33.8 0.0 copy-start.6
  33.8 0.0 copy-start.7
  33.8 20.9 %all_to_all.21.incoming = bf16[128,2,1664]{2,1,0:T(2,128)(2,1)S(1)} all-to-all(bf16[128,2,1664]{2,1,0:T(2,128)(2,1)S(1)} %bitcast.21), channel_id=1, replica_groups=mesh['x'=4,'y'=4,'z'=4,'core'=2] {'y','z','core','x'}, dimensions={0} | all-to-all | bytes 1703936 | tf_op jit(solution)/shard_map/all_to_all | solution.py:327
  54.8 0.0 copy-done.2
  54.8 0.0 copy-done.3
  54.8 0.0 copy-done.4
  54.8 0.0 copy-done.5
  54.8 0.0 copy-done.6
  54.8 0.8 shard_map.138
  55.6 20.8 %all_to_all.22 = bf16[128,2,1664]{2,1,0:T(2,128)(2,1)S(1)} all-to-all(bf16[128,2,1664]{2,1,0:T(2,128)(2,1)S(1)} %get-tuple-element.27), channel_id=1, replica_groups=mesh['x'=4,'y'=4,'z'=4,'core'=2] {'y','z','core','x'}, dimensions={0} | all-to-all | bytes 1703936 | tf_op jit(solution)/shard_map/all_to_all | solution.py:318
  76.5 2.3 %shard_map.139 = bf16[4,8,4,2,1664]{4,3,2,1,0:T(2,128)(2,1)S(1)} custom-call(bf16[4,8,4,2,1664]{4,3,2,1,0:T(2,128)(2,1)S(1)} %bitcast.18, s32[16,2]{1,0:T(8,128)S(1)} %get-tuple-element.24.mine, s32[2,16]{1,0:T(2,128)S(1)} %get-tuple-element.25.mine_t, bf16[3,16,12288]{2,1,0:T(8,128)(2,1)S(1)} %bitcast.17, bf16[16,12288]{1,0:T(8,128)(2,1)S(1)} %copy-done.1), custom_call_target="tpu_custom_call" | custom-call | tf_op jit(solution)/shard_map/pallas_call | solution.py:319
  78.8 20.8 %all_to_all.23.incoming = bf16[128,2,1664]{2,1,0:T(2,128)(2,1)S(1)} all-to-all(bf16[128,2,1664]{2,1,0:T(2,128)(2,1)S(1)} %bitcast.19), channel_id=1, replica_groups=mesh['x'=4,'y'=4,'z'=4,'core'=2] {'y','z','core','x'}, dimensions={0} | all-to-all | bytes 1703936 | tf_op jit(solution)/shard_map/all_to_all | solution.py:327
  99.6 1.6 %shard_map.140 = (f32[64,1536]{1,0:T(8,128)}, f32[64,1536]{1,0:T(8,128)}, f32[64,1536]{1,0:T(8,128)}, f32[8,13]{1,0:T(8,128)}, f32[8,13]{1,0:T(8,128)}, /*index=5*/f32[8,13]{1,0:T(8,128)}) custom-call(bf16[128,2,1664]{2,1,0:T(2,128)(2,1)S(1)} %all_to_all.23.incoming, bf16[256,64]{1,0:T(8,128)(2,1)S(1)} %get-tuple-element.26.picker, ...), custom_call_target="tpu_custom_call" | custom-call | tf_op jit(solution)/shard_map/pallas_call | solution.py:331
  (1 shorter events, 0.0 us)
Async XLA Ops:
  0.6 30.8 %copy-start.1 = (bf16[16,12288]{1,0:T(8,128)(2,1)S(1)}, bf16[16,12288]{1,0:T(8,128)(2,1)}, u32[]{:S(2)}) copy-start(bf16[16,12288]{1,0:T(8,128)(2,1)} %conf.3) | copy-start | bytes 1179652
  0.6 30.8 %copy-start = (bf16[16,3,12288]{2,0,1:T(8,128)(2,1)S(1)}, bf16[16,3,12288]{2,0,1:T(8,128)(2,1)}, u32[]{:S(2)}) copy-start(bf16[16,3,12288]{2,0,1:T(8,128)(2,1)} %param.16) | copy-start | bytes 3538948
  33.8 21.0 %copy-start.2 = (f32[64,1536]{1,0:T(8,128)S(1)}, f32[64,1536]{1,0:T(8,128)}, u32[]{:S(2)}) copy-start(f32[64,1536]{1,0:T(8,128)} %depth.1) | copy-start | bytes 1179652
  33.8 21.0 %copy-start.3 = (f32[64,1536]{1,0:T(8,128)S(1)}, f32[64,1536]{1,0:T(8,128)}, u32[]{:S(2)}) copy-start(f32[64,1536]{1,0:T(8,128)} %m.1) | copy-start | bytes 1179652
  33.8 21.0 %copy-start.4 = (f32[64,1536]{1,0:T(8,128)S(1)}, f32[64,1536]{1,0:T(8,128)}, u32[]{:S(2)}) copy-start(f32[64,1536]{1,0:T(8,128)} %v.1) | copy-start | bytes 1179652
  33.8 21.0 %copy-start.5 = (f32[13,8]{0,1:T(8,128)S(1)}, f32[13,8]{0,1:T(8,128)}, u32[]{:S(2)}) copy-start(f32[13,8]{0,1:T(8,128)} %param.12) | copy-start | bytes 1252
  33.8 21.0 %copy-start.6 = (f32[13,8]{0,1:T(8,128)S(1)}, f32[13,8]{0,1:T(8,128)}, u32[]{:S(2)}) copy-start(f32[13,8]{0,1:T(8,128)} %param.13) | copy-start | bytes 1252
  33.8 21.0 %copy-start.7 = (f32[13,8]{0,1:T(8,128)S(1)}, f32[13,8]{0,1:T(8,128)}, u32[]{:S(2)}) copy-start(f32[13,8]{0,1:T(8,128)} %param.14) | copy-start | bytes 1252

commit v7 on v4

--- a/solution.py
+++ b/solution.py
@@ -15,8 +15,9 @@
 LANES = 128
 CAP = 2
 CORES = 2
-SHARDS = 8
-ORDER = ("z", "x", "y", "core")
+SIDE = 4
+SHARDS = SIDE * CORES
+ORDER = ("core", "x", "y", "z")
 
 learn_rate = 0.01
 beta_first = 0.9
@@ -59,10 +60,9 @@
     value = jnp.where((local >= 0) & (local < views), local + 1, 0).astype(f32).astype(bf16)
     row = iota((slots, LANES), 0)
     lane = iota((slots, LANES), 1)
-    spread = dot(hot(row[:, :lines] // (CAP * CORES) % lines == lane[:, :lines]), value)
     place = row // CAP
-    shard = place // (CORES * lines) * CORES + place % CORES
-    hit = (spread > 0.5) & (lane // 16 == shard)
+    spread = dot(hot(place[:, :lines] // SIDE % lines == lane[:, :lines]), value)
+    hit = (spread > 0.5) & (lane // 16 == place % SIDE * CORES + place // (lines * SIDE))
     tri = hot(iota((LANES, LANES), 0) < iota((LANES, LANES), 1))
     rank = dot(hot(hit), tri)
     mine = hit & (rank == (row % CAP).astype(f32))
@@ -146,15 +146,15 @@
 
 
 def edge_kernel(arrived, mine, mine_t, points, conf, out, depth_s, grad_s):
-    planes, groups, cores, cap, width = arrived.shape
-    shards = planes * cores
+    cores, groups, side, cap, width = arrived.shape
+    shards = cores * side
     pixels = width - LANES
     edges = mine.shape[0]
     slots = shards * groups * cap
 
     def place(view):
         shard = view // 8 % shards
-        return (shard // cores * groups + view // (8 * shards)) * cores + shard % cores
+        return (shard % cores * groups + view // (8 * shards)) * side + shard // cores
 
     both = jnp.concatenate([mine[:, 0:1], mine[:, 1:2]], axis=0)
     pose_rows = arrived[:, :, :, :, pixels:].reshape(slots, LANES)
@@ -173,7 +173,7 @@
     slot = jnp.sum(jnp.where((group == group_row) & earlier, 1.0, 0.0), axis=1, keepdims=True)
     sel = hot((group * cap).astype(f32) + slot == iota((edges, groups * cap), 1).astype(f32))
     for s in range(shards):
-        rows = arrived[s // cores, :, s % cores, :, :pixels].reshape(groups * cap, pixels)
+        rows = arrived[s % cores, :, s // cores, :, :pixels].reshape(groups * cap, pixels)
         depth_s[:, s * pixels : (s + 1) * pixels] = jnp.exp(dot(sel, rows))
 
     pf = [poses[:edges, k : k + 1] for k in range(12)]
@@ -226,7 +226,7 @@
         for i in range(steps // shards):
             sums = step(s * (steps // shards) + i, sums)
         placed = dot(sel, grad_s[:, s * pixels : (s + 1) * pixels], ((0,), (0,))).astype(bf16)
-        out[s // cores, :, s % cores, :, :pixels] = placed.reshape(groups, cap, pixels)
+        out[s % cores, :, s // cores, :, :pixels] = placed.reshape(groups, cap, pixels)
 
     def total(x):
         return jnp.sum(x, axis=1, keepdims=True)
@@ -268,7 +268,7 @@
     both_row = jnp.concatenate([mine_t[0:1, :], mine_t[1:2, :]], axis=1)
     owner_hot = hot(iota((slots, 2 * edges), 0) // cap == place(both_row))
     owned = dot(owner_hot, lead) + dot(owner_hot, rest)
-    out[:, :, :, :, pixels:] = two_parts(owned).reshape(planes, groups, cores, cap, LANES)
+    out[:, :, :, :, pixels:] = two_parts(owned).reshape(cores, groups, side, cap, LANES)
 
 
 def call(kernel, outs, scratch=(), in_specs=None, mib=40):
@@ -310,14 +310,14 @@
             pltpu.SemaphoreType.DMA((3,)),
         ],
         [hbm, hbm, hbm],
-        64,
-    )(pairs.T.reshape(2, -1, LANES).transpose(1, 0, 2), log_depth, poses[0])
+        40,
+    )(*[pltpu.with_memory_space_constraint(x, pltpu.HBM) for x in (pairs.T.reshape(2, -1, LANES).transpose(1, 0, 2), log_depth, poses[0])])
     planes = points.transpose(1, 0, 2)
     for turn in range(ITERS):
-        arrived = exchange(sending).reshape(n_edge // CORES, n_view, CORES, CAP, width)
+        arrived = exchange(sending).reshape(CORES, n_view, SIDE, CAP, width)
         back = call(
             edge_kernel,
-            S((n_edge // CORES, n_view, CORES, CAP, width), bf16),
+            S((CORES, n_view, SIDE, CAP, width), bf16),
             [
                 pltpu.VMEM((edges, pixels * n_edge), f32),
                 pltpu.VMEM((edges, pixels * n_edge), bf16),
@@ -337,7 +337,7 @@
 
 
 def solution(mesh):
-    grid = jax.sharding.Mesh(mesh.devices.reshape(4, 4, SHARDS // CORES, CORES), ("x", "y", "z", "core"))
+    grid = jax.sharding.Mesh(mesh.devices.reshape(SIDE, SIDE, SIDE, CORES), ("x", "y", "z", "core"))
     view, edge = ("x", "y"), ("z", "core")
     depth = P(view, edge)
     pose = P(None, view + edge)

time: 103 us -> 100 us (0.971)
  blocking collectives: 92.2 us -> 90.4 us
    all_to_all x2, blocking collectives: 49.6 us -> 48.3 us  [shards(): arrived = exchange(sending).reshape(CORES, n_view, SIDE, CAP, width)]
where the time goes in v7:
time: 100 us
  blocking collectives  90.4 us (90%)
  Pallas kernels  8.87 us (9%)
    all_to_all x2, blocking collectives, shards(): arrived = exchange(sending).reshape(CORES, n_view, SIDE, CAP, width)  48.3 us
    all_to_all x2, blocking collectives, shards(): incoming = exchange(back.reshape(owners, CAP, width))  42.1 us
    pallas_call x2, Pallas kernels, shards(): call(edge_kernel, S((CORES, n_view, SIDE, CAP, width), bf16), [pltpu.VMEM...  4.67 us
    pallas_call x2, Pallas kernels, shards(): call(kernel, depth_out + pose_out + ([] if last else [message]))  2.39 us

profile of v7, /device:TPU:1, one launch (start us, length us, event | category | flops | bytes accessed | tf_op | source)
XLA Modules:
  0.0 100.1 jit_solution(3629585722689196167)
XLA Ops:
  0.6 0.0 copy-start.1
  0.6 0.0 copy-start
  0.7 1.8 %shard_map.136 = (bf16[128,2,1664]{2,1,0:T(2,128)(2,1)S(1)}, bf16[256,64]{1,0:T(8,128)(2,1)S(1)}, s32[16,2]{1,0:T(8,128)S(1)}, s32[2,16]{1,0:T(2,128)S(1)}) custom-call(s32[16,2,128]{2,1,0:T(2,128)} %bitcast.26, f32[64,1536]{1,0:T(8,128)} %depth.1, f32[8,13]{1,0:T(8,128)} %bitcast.22), custom_call_target="tpu_custom_call" | custom-call | tf_op jit(solution)/shard_map/pallas_call | solution.py:303
  2.5 27.3 %all_to_all.20 = bf16[128,2,1664]{2,1,0:T(2,128)(2,1)S(1)} all-to-all(bf16[128,2,1664]{2,1,0:T(2,128)(2,1)S(1)} %get-tuple-element.23), channel_id=1, replica_groups=mesh['x'=4,'y'=4,'z'=4,'core'=2] {'core','x','y','z'}, dimensions={0} | all-to-all | bytes 1703936 | tf_op jit(solution)/shard_map/all_to_all | solution.py:317
  29.7 0.0 copy-done.1
  29.7 0.0 copy-done
  29.7 2.3 %shard_map.137 = bf16[2,16,4,2,1664]{4,3,2,1,0:T(2,128)(2,1)S(1)} custom-call(bf16[2,16,4,2,1664]{4,3,2,1,0:T(2,128)(2,1)S(1)} %bitcast.20, s32[16,2]{1,0:T(8,128)S(1)} %get-tuple-element.24.mine, s32[2,16]{1,0:T(2,128)S(1)} %get-tuple-element.25.mine_t, bf16[3,16,12288]{2,1,0:T(8,128)(2,1)S(1)} %bitcast.16, bf16[16,12288]{1,0:T(8,128)(2,1)S(1)} %copy-done.1), custom_call_target="tpu_custom_call" | custom-call | tf_op jit(solution)/shard_map/pallas_call | solution.py:318
  32.1 0.0 copy-start.2
  32.1 0.0 copy-start.3
  32.1 0.0 copy-start.4
  32.1 0.0 copy-start.5
  32.1 0.0 copy-start.6
  32.1 0.0 copy-start.7
  32.2 21.1 %all_to_all.21.incoming = bf16[128,2,1664]{2,1,0:T(2,128)(2,1)S(1)} all-to-all(bf16[128,2,1664]{2,1,0:T(2,128)(2,1)S(1)} %bitcast.21), channel_id=1, replica_groups=mesh['x'=4,'y'=4,'z'=4,'core'=2] {'core','x','y','z'}, dimensions={0} | all-to-all | bytes 1703936 | tf_op jit(solution)/shard_map/all_to_all | solution.py:326
  53.2 0.0 copy-done.2
  53.2 0.0 copy-done.3
  53.2 0.0 copy-done.4
  53.2 0.0 copy-done.5
  53.2 0.0 copy-done.6
  53.3 0.8 shard_map.138
  54.1 21.1 %all_to_all.22 = bf16[128,2,1664]{2,1,0:T(2,128)(2,1)S(1)} all-to-all(bf16[128,2,1664]{2,1,0:T(2,128)(2,1)S(1)} %get-tuple-element.27), channel_id=1, replica_groups=mesh['x'=4,'y'=4,'z'=4,'core'=2] {'core','x','y','z'}, dimensions={0} | all-to-all | bytes 1703936 | tf_op jit(solution)/shard_map/all_to_all | solution.py:317
  75.1 2.3 %shard_map.139 = bf16[2,16,4,2,1664]{4,3,2,1,0:T(2,128)(2,1)S(1)} custom-call(bf16[2,16,4,2,1664]{4,3,2,1,0:T(2,128)(2,1)S(1)} %bitcast.18, s32[16,2]{1,0:T(8,128)S(1)} %get-tuple-element.24.mine, s32[2,16]{1,0:T(2,128)S(1)} %get-tuple-element.25.mine_t, bf16[3,16,12288]{2,1,0:T(8,128)(2,1)S(1)} %bitcast.17, bf16[16,12288]{1,0:T(8,128)(2,1)S(1)} %copy-done.1), custom_call_target="tpu_custom_call" | custom-call | tf_op jit(solution)/shard_map/pallas_call | solution.py:318
  77.5 21.1 %all_to_all.23.incoming = bf16[128,2,1664]{2,1,0:T(2,128)(2,1)S(1)} all-to-all(bf16[128,2,1664]{2,1,0:T(2,128)(2,1)S(1)} %bitcast.19), channel_id=1, replica_groups=mesh['x'=4,'y'=4,'z'=4,'core'=2] {'core','x','y','z'}, dimensions={0} | all-to-all | bytes 1703936 | tf_op jit(solution)/shard_map/all_to_all | solution.py:326
  98.5 1.6 %shard_map.140 = (f32[64,1536]{1,0:T(8,128)}, f32[64,1536]{1,0:T(8,128)}, f32[64,1536]{1,0:T(8,128)}, f32[8,13]{1,0:T(8,128)}, f32[8,13]{1,0:T(8,128)}, /*index=5*/f32[8,13]{1,0:T(8,128)}) custom-call(bf16[128,2,1664]{2,1,0:T(2,128)(2,1)S(1)} %all_to_all.23.incoming, bf16[256,64]{1,0:T(8,128)(2,1)S(1)} %get-tuple-element.26.picker, ...), custom_call_target="tpu_custom_call" | custom-call | tf_op jit(solution)/shard_map/pallas_call | solution.py:330
  (1 shorter events, 0.0 us)
Async XLA Ops:
  0.6 29.1 %copy-start.1 = (bf16[16,12288]{1,0:T(8,128)(2,1)S(1)}, bf16[16,12288]{1,0:T(8,128)(2,1)}, u32[]{:S(2)}) copy-start(bf16[16,12288]{1,0:T(8,128)(2,1)} %conf.3) | copy-start | bytes 1179652
  0.6 29.1 %copy-start = (bf16[16,3,12288]{2,0,1:T(8,128)(2,1)S(1)}, bf16[16,3,12288]{2,0,1:T(8,128)(2,1)}, u32[]{:S(2)}) copy-start(bf16[16,3,12288]{2,0,1:T(8,128)(2,1)} %param.16) | copy-start | bytes 3538948
  32.1 21.1 %copy-start.2 = (f32[64,1536]{1,0:T(8,128)S(1)}, f32[64,1536]{1,0:T(8,128)}, u32[]{:S(2)}) copy-start(f32[64,1536]{1,0:T(8,128)} %depth.1) | copy-start | bytes 1179652
  32.1 21.1 %copy-start.3 = (f32[64,1536]{1,0:T(8,128)S(1)}, f32[64,1536]{1,0:T(8,128)}, u32[]{:S(2)}) copy-start(f32[64,1536]{1,0:T(8,128)} %m.1) | copy-start | bytes 1179652
  32.1 21.1 %copy-start.4 = (f32[64,1536]{1,0:T(8,128)S(1)}, f32[64,1536]{1,0:T(8,128)}, u32[]{:S(2)}) copy-start(f32[64,1536]{1,0:T(8,128)} %v.1) | copy-start | bytes 1179652
  32.1 21.1 %copy-start.5 = (f32[13,8]{0,1:T(8,128)S(1)}, f32[13,8]{0,1:T(8,128)}, u32[]{:S(2)}) copy-start(f32[13,8]{0,1:T(8,128)} %param.12) | copy-start | bytes 1252
  32.1 21.1 %copy-start.6 = (f32[13,8]{0,1:T(8,128)S(1)}, f32[13,8]{0,1:T(8,128)}, u32[]{:S(2)}) copy-start(f32[13,8]{0,1:T(8,128)} %param.13) | copy-start | bytes 1252
  32.1 21.1 %copy-start.7 = (f32[13,8]{0,1:T(8,128)S(1)}, f32[13,8]{0,1:T(8,128)}, u32[]{:S(2)}) copy-start(f32[13,8]{0,1:T(8,128)} %param.14) | copy-start | bytes 1252
